TPU v7x, 128 devices: a whole 4x4x4 slice. The times are simulated.
128 devices in a mesh: row: 8 (over y, core), col: 16 (over z, x).
Axes of the slice: x: 4, y: 4, z: 4, core: 2. Of those that a mesh axis runs over, the one named last changes fastest.
Arguments:
- amplitudes: bfloat16 [6144, 2048], P(('row', 'col')), may hold values from -6 to 6
- integrals: bfloat16 [128, 16, 8, 128, 128], P(('row', 'col')), may hold values from -0.25 to 0.25
- slot_index: int32 [128, 16, 8, 2], P(('row', 'col')), may hold values from 0 to 47, as said below
- virt_energy: float32 [3072], P(('row', 'col')), may hold values from 0.3 to 3
- b_energy: float32 [2], replicated, may hold values from 0.3 to 3
- pair_energy: float32 [2048], replicated, may hold values from -3 to -0.5
Outputs:
- update: float32 [2, 3072, 2048], P(None, ('row', 'col'))
Inputs may be any that keep to these rules, and one draw needn't show every extreme that they name: `slot_index`: A device sends at most 8 filled slots to each member of its row group, filled slots first; in every row group one member receives 8 filled slots from every device of the group, and one device holds 8 filled slots for every member; filled and empty slots both occur.
All inputs are finite; a program needn't handle non-finite values.
Results may differ from a plain program's by a relative error of at most 0.0003.
Values may be sent and summed in bfloat16 or wider, within the bound.
A program may use at most 128 MiB of HBM per device.

v0:
```python
import jax
import jax.numpy as jnp
from jax import lax
from jax.sharding import PartitionSpec as P

NT = 24
NB = 2


def per_device(amplitudes, integrals, slot_index, virt_energy, b_energy, pair_energy):
    whole = lax.all_gather(amplitudes, ("row", "col"), axis=0, tiled=True)
    tile = integrals.shape[-1]
    pairs = whole.shape[1]
    amp_tiles = whole.reshape(-1, tile, pairs)
    a_local = NT // lax.axis_size("row")
    moved, moved_index = (
        lax.all_to_all(integrals, "col", split_axis=1, concat_axis=1, tiled=True),
        lax.all_to_all(slot_index, "col", split_axis=1, concat_axis=1, tiled=True),
    )
    member_tiles = moved[0]
    member_index = moved_index[0]
    empty_mark = NB * a_local
    filled = jnp.sum((member_index[:, :, 0] != empty_mark).astype(jnp.int32), axis=1)

    def per_member(member, partial_value):

        def per_slot(slot, acc):
            out_block = member_index[member, slot, 0]
            amp_block = member_index[member, slot, 1]
            tile_now = member_tiles[member, slot]
            operand = lax.dynamic_index_in_dim(amp_tiles, amp_block, 0, keepdims=False)
            contrib = jnp.dot(tile_now, operand, preferred_element_type=jnp.float32)
            current = lax.dynamic_index_in_dim(acc, out_block, 0, keepdims=False)
            return lax.dynamic_update_index_in_dim(acc, current + contrib, out_block, 0)

        return lax.fori_loop(0, filled[member], per_slot, partial_value)

    start = jnp.zeros((NB * a_local, tile, pairs), jnp.float32)
    partial_value = lax.fori_loop(0, member_tiles.shape[0], per_member, start)
    ladder_rows = partial_value.reshape(NB, a_local * tile, pairs)
    owned = lax.psum_scatter(ladder_rows, "col", scatter_dimension=1, tiled=True)
    denom = virt_energy[None, :, None] + b_energy[:, None, None] - pair_energy[None, None, :]
    return owned / denom


def solution(mesh):
    placed = (
        P(("row", "col"), None),
        P(("row", "col"), None, None, None, None),
        P(("row", "col"), None, None, None),
        P(("row", "col")),
        P(),
        P(),
    )
    return jax.shard_map(
        per_device,
        mesh=mesh,
        in_specs=placed,
        out_specs=P(None, ("row", "col"), None),
        check_vma=False,
    )
```

profile of v0, /device:TPU:1, one launch (start us, length us, event | category | flops | bytes accessed | tf_op | source)
XLA Modules:
  0.0 1407.3 jit_solution(13353710490797846651)
XLA Ops:
  8.0 14.7 %all_to_all.10 = s32[1,16,8,2]{2,3,0,1:T(2,128)S(1)} all-to-all(s32[1,16,8,2]{2,3,0,1:T(2,128)S(1)} %copy.10), channel_id=1, replica_groups=mesh['row'=8,'col'=16] {'col'}, dimensions={1} | all-to-all | bytes 2048 | tf_op jit(solution)/shard_map/all_to_all | solution.py:18
  22.7 4.6 all-to-all-start.1
  27.8 67.5 %all-to-all-done.1 = bf16[1,16,8,128,128]{4,3,2,0,1:T(8,128)(2,1)} async-done(((bf16[1,16,8,128,128]{4,3,2,0,1:T(8,128)(2,1)}), bf16[1,16,8,128,128]{4,3,2,0,1:T(8,128)(2,1)}, u32[]{:S(2)}, u32[]{:S(2)}) %all-to-all-start.1) | async-done | bytes 4194336 | tf_op jit(solution)/shard_map/all_to_all | solution.py:17
  95.3 49.2 %all-gather.2.cloned.1.call-done = bf16[6144,2048]{1,0:T(8,128)(2,1)} async-done(((bf16[48,2048]{1,0:T(8,128)(2,1)}), bf16[6144,2048]{1,0:T(8,128)(2,1)}) %all-gather.2.cloned.1.call-update) | async-done | bytes 25165840 | tf_op jit(solution)/shard_map/all_gather | solution.py:11
  144.5 3.5 broadcast_in_dim.12
  148.0 309.5 %while.36 = (s32[]{:T(128)}, f32[6,128,2048]{2,1,0:T(8,128)}, s32[16]{0:T(128)S(1)}, s32[16,8,2]{0,2,1:T(2,128)S(1)}, bf16[16,8,128,128]{3,2,1,0:T(8,128)(2,1)},...) while((s32[]{:T(128)}, f32[6,128,2048]{2,1,0:T(8,128)}, ...), condition=%wide.region_4.5_spmd, body=%wide.region_1.4_spmd.sunk | while | flops 67371016 | bytes 4752372 | solution.py:39
  148.6 9.6 while.37
  160.3 18.6 %while.37 = (s32[]{:T(128)}, f32[6,128,2048]{2,1,0:T(8,128)}, s32[]{:T(128)}, s32[16,8,2]{0,2,1:T(2,128)S(1)}, s32[]{:T(128)}, /*index=5*/bf16[16,8,128,128]{3,2...) while((s32[]{:T(128)}, f32[6,128,2048]{2,1,0:T(8,128)}, ...), condition=%wide.region_3.3_spmd, body=%wide.region_2.2_spmd.sunk | while | flops 67371016 | bytes 4752131 | solution.py:36
  179.6 72.6 %while.37 = (s32[]{:T(128)}, f32[6,128,2048]{2,1,0:T(8,128)}, s32[]{:T(128)}, s32[16,8,2]{0,2,1:T(2,128)S(1)}, s32[]{:T(128)}, /*index=5*/bf16[16,8,128,128]{3,2...) while((s32[]{:T(128)}, f32[6,128,2048]{2,1,0:T(8,128)}, ...), condition=%wide.region_3.3_spmd, body=%wide.region_2.2_spmd.sunk | while | flops 67371016 | bytes 4752131 | solution.py:36
  195.2 2.4 fusion.13
  252.8 9.7 while.37
  263.2 27.8 %while.37 = (s32[]{:T(128)}, f32[6,128,2048]{2,1,0:T(8,128)}, s32[]{:T(128)}, s32[16,8,2]{0,2,1:T(2,128)S(1)}, s32[]{:T(128)}, /*index=5*/bf16[16,8,128,128]{3,2...) while((s32[]{:T(128)}, f32[6,128,2048]{2,1,0:T(8,128)}, ...), condition=%wide.region_3.3_spmd, body=%wide.region_2.2_spmd.sunk | while | flops 67371016 | bytes 4752131 | solution.py:36
  269.8 2.4 fusion.13
  291.6 9.7 while.37
  303.3 9.7 while.37
  315.0 27.7 %while.37 = (s32[]{:T(128)}, f32[6,128,2048]{2,1,0:T(8,128)}, s32[]{:T(128)}, s32[16,8,2]{0,2,1:T(2,128)S(1)}, s32[]{:T(128)}, /*index=5*/bf16[16,8,128,128]{3,2...) while((s32[]{:T(128)}, f32[6,128,2048]{2,1,0:T(8,128)}, ...), condition=%wide.region_3.3_spmd, body=%wide.region_2.2_spmd.sunk | while | flops 67371016 | bytes 4752131 | solution.py:36
  343.3 36.7 %while.37 = (s32[]{:T(128)}, f32[6,128,2048]{2,1,0:T(8,128)}, s32[]{:T(128)}, s32[16,8,2]{0,2,1:T(2,128)S(1)}, s32[]{:T(128)}, /*index=5*/bf16[16,8,128,128]{3,2...) while((s32[]{:T(128)}, f32[6,128,2048]{2,1,0:T(8,128)}, ...), condition=%wide.region_3.3_spmd, body=%wide.region_2.2_spmd.sunk | while | flops 67371016 | bytes 4752131 | solution.py:36
  380.7 9.7 while.37
  387.3 2.4 fusion.13
  391.1 36.6 %while.37 = (s32[]{:T(128)}, f32[6,128,2048]{2,1,0:T(8,128)}, s32[]{:T(128)}, s32[16,8,2]{0,2,1:T(2,128)S(1)}, s32[]{:T(128)}, /*index=5*/bf16[16,8,128,128]{3,2...) while((s32[]{:T(128)}, f32[6,128,2048]{2,1,0:T(8,128)}, ...), condition=%wide.region_3.3_spmd, body=%wide.region_2.2_spmd.sunk | while | flops 67371016 | bytes 4752131 | solution.py:36
  397.7 2.4 fusion.13
  428.4 18.7 %while.37 = (s32[]{:T(128)}, f32[6,128,2048]{2,1,0:T(8,128)}, s32[]{:T(128)}, s32[16,8,2]{0,2,1:T(2,128)S(1)}, s32[]{:T(128)}, /*index=5*/bf16[16,8,128,128]{3,2...) while((s32[]{:T(128)}, f32[6,128,2048]{2,1,0:T(8,128)}, ...), condition=%wide.region_3.3_spmd, body=%wide.region_2.2_spmd.sunk | while | flops 67371016 | bytes 4752131 | solution.py:36
  447.7 9.7 while.37
  458.2 940.4 %reduce-scatter.2.cloned.1.call-done = f32[2,24,2048]{2,1,0:T(8,128)} async-done(((f32[2,384,2048]{2,1,0:T(8,128)}), f32[2,24,2048]{2,1,0:T(8,128)}) %reduce-scatter.2.cloned.1.call-update) | async-done | bytes 393232 | tf_op jit(solution)/shard_map/reduce_scatter | solution.py:41
  (126 shorter events, 146.4 us)
Async XLA Ops:
  6.5 138.0 %all-gather.2.cloned.1.call-start = ((), (), s32[]{:S(2)}) async-start(), calls=%async_computation.3 | async-start | bytes 25362432 | tf_op jit(solution)/shard_map/all_gather | solution.py:11
  22.7 72.6 %all-to-all-start.1 = ((bf16[1,16,8,128,128]{4,3,2,0,1:T(8,128)(2,1)}), bf16[1,16,8,128,128]{4,3,2,0,1:T(8,128)(2,1)}, u32[]{:S(2)}, u32[]{:S(2)}) async-start(bf16[1,16,8,128,128]{4,3,2,0,1:T(8,128)(2,1)} %bitcast.36), calls=%async_computation.1 | async-start | bytes 8388608 | tf_op jit(solution)/shard_map/all_to_all | solution.py:17
  27.3 1371.3 %reduce-scatter.2.cloned.1.call-start = ((), (), s32[]{:S(2)}) async-start(), calls=%async_computation.4 | async-start | bytes 6684672 | tf_op jit(solution)/shard_map/reduce_scatter | solution.py:41
  457.4 0.7 copy-start.1
  457.5 0.7 copy-start.2
  457.5 941.1 %copy-start = (f32[2048]{0:T(1024)S(1)}, f32[2048]{0:T(1024)}, u32[]{:S(2)}) copy-start(f32[2048]{0:T(1024)} %param.15) | copy-start | bytes 24580
Sparse Core Ops, SparseCore 0:
  10.4 134.0 all-gather.1
  457.6 940.9 reduce-scatter.1
where the time goes:
time: 1420 us; the launch traced here: 1410 us
  waiting for transfers between devices  1060 us (75%)
  loops' own time  160 us (11%)
  local copies, waits for them, and re-layouts  78.7 us (6%)
  matrix products  75.8 us (5%)
  blocking collectives  14.7 us (1%)
    reduce_scatter x1, waiting for transfers between devices, per_device(): lax.psum_scatter(ladder_rows, 'col', scatter_dimension=1, tiled=True)  940 us
    another operation x16, loops' own time, per_member(): return lax.fori_loop(0, filled[member], per_slot, partial_value)  160 us
    dot_general x32, matrix products, per_slot(): contrib = jnp.dot(tile_now, operand, preferred_element_type=jnp.float32)  75.8 us
    all_to_all x1, waiting for transfers between devices, per_device(): lax.all_to_all(integrals, 'col', split_axis=1, concat_axis=1, tiled=True)  67.5 us
    all_gather x1, waiting for transfers between devices, per_device(): whole = lax.all_gather(amplitudes, ('row', 'col'), axis=0, tiled=True)  49.2 us
    dynamic_slice x32, local copies, waits for them, and re-layouts, per_slot(): current = lax.dynamic_index_in_dim(acc, out_block, 0, keepdims=False)  41.6 us
  transfers between devices with their start and end apart: 3, of which 3 were waited for; matrix products, arithmetic and copies ran while one was open for 0% of the time, Pallas kernels for 0%

commit v1 on v0

v1 whole, which is shorter than its diff:
```python
import jax
import jax.numpy as jnp
from jax import lax
from jax.experimental import pallas as pl
from jax.experimental.pallas import tpu as pltpu
from jax.sharding import PartitionSpec as P

NT = 24
NB = 2
TILE = 128
GROUP = 4
WIDTH = 512


def slot_kernel(n_out, n_slot, out_idx, amp_idx, tiles, amps, partial, order, amp_of, first, fill):
    @pl.when(pl.program_id(0) == 0)
    def _():
        for o in range(n_out + 1):
            fill[o] = 0

        def count(s, carry):
            o = out_idx[s]
            fill[o] = fill[o] + 1
            return carry

        lax.fori_loop(0, n_slot, count, 0)
        start = jnp.int32(0)
        for o in range(n_out):
            first[o] = start
            start = start + lax.div(fill[o] + (GROUP - 1), GROUP)
            fill[o] = first[o] * GROUP
        first[n_out] = start
        fill[n_out] = start * GROUP

        def blank(p, carry):
            order[p] = n_slot
            amp_of[p] = 0
            return carry

        lax.fori_loop(0, start * GROUP, blank, 0)

        def place(s, carry):
            o = out_idx[s]

            @pl.when(o < n_out)
            def _():
                p = fill[o]
                order[p] = s
                amp_of[p] = amp_idx[s]
                fill[o] = p + 1

            return carry

        lax.fori_loop(0, n_slot, place, 0)

    for o in range(n_out):
        partial[o] = jnp.zeros(partial.shape[1:], jnp.float32)

        def step(q, carry):
            left = []
            for g in range(GROUP):
                s = order[q * GROUP + g]
                tile = tiles[lax.min(s, n_slot - 1)]
                left.append(jnp.where(s < n_slot, tile, jnp.zeros_like(tile)))
            right = [amps[amp_of[q * GROUP + g]] for g in range(GROUP)]
            partial[o] += jnp.dot(
                jnp.concatenate(left, axis=1), jnp.concatenate(right, axis=0), preferred_element_type=jnp.float32
            )
            return carry

        lax.fori_loop(first[o], first[o + 1], step, 0)


def slot_products(tiles, out_idx, amp_idx, amps):
    n_slot = tiles.shape[0]
    n_out = NB * 3
    pairs = amps.shape[2]
    room = n_slot + n_out * GROUP

    def kern(oi, ai, t, a, p, *scratch):
        slot_kernel(n_out, n_slot, oi, ai, t, a, p, *scratch)

    return pl.pallas_call(
        kern,
        grid=(pairs // WIDTH,),
        out_shape=jax.ShapeDtypeStruct((n_out, TILE, pairs), jnp.float32),
        in_specs=[
            pl.BlockSpec(memory_space=pltpu.SMEM),
            pl.BlockSpec(memory_space=pltpu.SMEM),
            pl.BlockSpec(memory_space=pltpu.VMEM),
            pl.BlockSpec((amps.shape[0], TILE, WIDTH), lambda i: (0, 0, i)),
        ],
        out_specs=pl.BlockSpec((n_out, TILE, WIDTH), lambda i: (0, 0, i)),
        scratch_shapes=[
            pltpu.SMEM((room,), jnp.int32),
            pltpu.SMEM((room,), jnp.int32),
            pltpu.SMEM((n_out + 1,), jnp.int32),
            pltpu.SMEM((n_out + 1,), jnp.int32),
        ],
        compiler_params=pltpu.CompilerParams(vmem_limit_bytes=56 * 1024 * 1024),
        name="slot_products",
    )(out_idx, amp_idx, tiles, amps)


def per_device(amplitudes, integrals, slot_index, virt_energy, b_energy, pair_energy):
    whole = lax.all_gather(amplitudes, ("row", "col"), axis=0, tiled=True)
    pairs = whole.shape[1]
    amp_tiles = whole.reshape(-1, TILE, pairs)
    a_local = NT // lax.axis_size("row")
    index = slot_index.reshape(-1, 2)
    tiles = integrals.reshape(-1, TILE, TILE)
    partial = slot_products(tiles, index[:, 0], index[:, 1], amp_tiles)
    ladder_rows = partial.reshape(NB, a_local * TILE, pairs)
    owned = lax.psum_scatter(ladder_rows, "col", scatter_dimension=1, tiled=True)
    denom = virt_energy[None, :, None] + b_energy[:, None, None] - pair_energy[None, None, :]
    return owned / denom


def solution(mesh):
    placed = (
        P(("row", "col"), None),
        P(("row", "col"), None, None, None, None),
        P(("row", "col"), None, None, None),
        P(("row", "col")),
        P(),
        P(),
    )
    return jax.shard_map(
        per_device,
        mesh=mesh,
        in_specs=placed,
        out_specs=P(None, ("row", "col"), None),
        check_vma=False,
    )
```

time: 1420 us -> 237 us (0.17)
  waiting for transfers between devices: 1060 us -> 195 us
  loops' own time: 160 us -> 0 us
  local copies, waits for them, and re-layouts: 78.7 us -> 2.08 us
  matrix products: 75.8 us -> 0 us
  Pallas kernels: 0 us -> 24.2 us
  blocking collectives: 14.7 us -> 0 us
    reduce_scatter x1, waiting for transfers between devices: 940 us -> 96 us  [per_device(): lax.psum_scatter(ladder_rows, 'col', scatter_dimension=1, tiled=True)]
    another operation x17 -> x0, loops' own time: 160 us -> none  [the longest x16 160 us: per_member(): return lax.fori_loop(0, filled[member], per_slot, partial_value)]
    dot_general x32 -> x0, matrix products: 75.8 us -> none  [per_slot(): contrib = jnp.dot(tile_now, operand, preferred_element_type=jnp.float32)]
    dynamic_slice x80 -> x0, local copies, waits for them, and re-layouts: 73.7 us -> none  [the longest x32 41.6 us: per_slot(): current = lax.dynamic_index_in_dim(acc, out_block, 0, keepdims=False)]
    all_to_all x1 -> x0, waiting for transfers between devices: 67.5 us -> none  [per_device(): lax.all_to_all(integrals, 'col', split_axis=1, concat_axis=1, tiled=True)]
    all_gather x1, waiting for transfers between devices: 49.2 us -> 98.4 us  [per_device(): whole = lax.all_gather(amplitudes, ('row', 'col'), axis=0, tiled=True)]
    pallas_call x0 -> x1, Pallas kernels: none -> 24.2 us  [slot_products(): pl.pallas_call(kern, grid=(pairs // WIDTH,), out_shape=jax.ShapeDtypeStru...]
    all_to_all x1 -> x0, blocking collectives: 14.7 us -> none  [per_device(): lax.all_to_all(slot_index, 'col', split_axis=1, concat_axis=1, tiled=True)]
  transfers between devices with their start and end apart: 3 -> 2, of which waited for: 3 -> 2; matrix products, arithmetic and copies ran while one was open for 0% -> 1% of each run, Pallas kernels for 0% -> 0%
where the time goes in v1:
time: 237 us
  waiting for transfers between devices  195 us (82%)
  Pallas kernels  24.2 us (10%)
  between operations  13.4 us (6%)
    all_gather x1, waiting for transfers between devices, per_device(): whole = lax.all_gather(amplitudes, ('row', 'col'), axis=0, tiled=True)  98.4 us
    reduce_scatter x1, waiting for transfers between devices, per_device(): lax.psum_scatter(ladder_rows, 'col', scatter_dimension=1, tiled=True)  96 us
    pallas_call x1, Pallas kernels, slot_products(): pl.pallas_call(kern, grid=(pairs // WIDTH,), out_shape=jax.ShapeDtypeStru...  24.2 us
  transfers between devices with their start and end apart: 2, of which 2 were waited for; matrix products, arithmetic and copies ran while one was open for 1% of the time, Pallas kernels for 0%

profile of v1, /device:TPU:1, one launch (start us, length us, event | category | flops | bytes accessed | tf_op | source)
XLA Modules:
  0.0 236.8 jit_solution(10621771259387875279)
XLA Ops:
  6.5 0.0 all-gather.2.cloned.1.call-start
  6.5 0.7 all-gather.2.cloned.1.call-update
  7.3 0.0 reduce-scatter.2.cloned.1.call-start
  7.3 0.8 copy.7
  8.1 0.1 reshape.45
  8.2 0.6 slice_bitcast_fusion
  8.7 98.4 %all-gather.2.cloned.1.call-done = bf16[6144,2048]{1,0:T(8,128)(2,1)} async-done(((bf16[48,2048]{1,0:T(8,128)(2,1)}), bf16[6144,2048]{1,0:T(8,128)(2,1)}) %all-gather.2.cloned.1.call-update) | async-done | bytes 25165840 | tf_op jit(solution)/shard_map/all_gather | solution.py:106
  107.2 24.2 %slot_products.1 = f32[6,128,2048]{2,1,0:T(8,128)} custom-call(s32[128]{0:T(128)} %get-tuple-element.6.oi, s32[128]{0:T(128)} %get-tuple-element.5.ai, bf16[128,128,128]{2,1,0:T(8,128)(2,1)} %bitcast.13, bf16[48,128,2048]{2,1,0:T(8,128)(2,1)} %bitcast.11), custom_call_target="tpu_custom_call" | custom-call | tf_op jit(solution)/shard_map/slot_products/pallas_call | solution.py:83
  131.4 0.0 copy-start.1
  131.4 0.0 copy-start.2
  131.4 0.0 copy-start
  131.4 0.0 reduce-scatter.2.cloned.1.call-update
  131.4 0.6 copy-done.1
  132.0 0.0 copy-done.2
  132.0 0.1 broadcast_add_fusion
  132.1 96.0 %reduce-scatter.2.cloned.1.call-done = f32[2,24,2048]{2,1,0:T(8,128)} async-done(((f32[2,384,2048]{2,1,0:T(8,128)}), f32[2,24,2048]{2,1,0:T(8,128)}) %reduce-scatter.2.cloned.1.call-update) | async-done | bytes 393232 | tf_op jit(solution)/shard_map/reduce_scatter | solution.py:114
  228.1 0.0 copy-done
  228.1 1.9 subtract_divide_fusion
Async XLA Ops:
  6.5 100.6 %all-gather.2.cloned.1.call-start = ((), (), s32[]{:S(2)}) async-start(), calls=%async_computation.1 | async-start | bytes 25362432 | tf_op jit(solution)/shard_map/all_gather | solution.py:106
  7.3 220.8 %reduce-scatter.2.cloned.1.call-start = ((), (), s32[]{:S(2)}) async-start(), calls=%async_computation.2 | async-start | bytes 6684672 | tf_op jit(solution)/shard_map/reduce_scatter | solution.py:114
  131.4 0.7 copy-start.1
  131.4 0.7 copy-start.2
  131.4 96.7 %copy-start = (f32[2048]{0:T(1024)S(1)}, f32[2048]{0:T(1024)}, u32[]{:S(2)}) copy-start(f32[2048]{0:T(1024)} %param.11) | copy-start | bytes 24580
Sparse Core Ops, SparseCore 0:
  10.4 96.6 all-gather.1
  131.5 96.5 reduce-scatter.1

commit v2 on v0

v2 whole, which is shorter than its diff:
```python
import functools

import jax
import jax.numpy as jnp
from jax import lax
from jax.experimental import pallas as pl
from jax.experimental.pallas import tpu as pltpu
from jax.sharding import PartitionSpec as P

MESH = pl.DeviceIdType.MESH
NT = 24
NB = 2
TILE = 128
SLOTS = 128
OUTS = 6
GROUP = 4
QUADS = 36
LANES = 128
SUBS = 8
CHUNKS = 4
WIDE = LANES * SUBS // CHUNKS
OWN = 24
ROWS = 48
RING = 4
Y, Z, X = 0, 1, 2
ORDERS = (
    (X, Z, Y), (Y, Z, X),
    (Z, X, Y), (Y, X, Z),
    (X, Z, Y), (Y, Z, X),
    (Z, X, Y), (Y, X, Z),
)
SUM_ORDERS = ((X, Z), (Z, X), (X, Z), (Z, X))


def list_kernel(out_idx, amp_idx, lists, fill, first):
    for o in range(OUTS + 1):
        fill[o] = 0

    def count(s, carry):
        o = out_idx[s]
        fill[o] = fill[o] + 1
        return carry

    lax.fori_loop(0, SLOTS, count, 0, unroll=4)

    def blank(q, carry):
        for g in range(GROUP):
            lists[g, q] = SLOTS
            lists[GROUP + g, q] = 0
        lists[0, 64 + q] = q
        return carry

    lax.fori_loop(0, QUADS, blank, 0, unroll=2)
    start = jnp.int32(0)
    for o in range(OUTS):
        here = lax.div(fill[o] + (GROUP - 1), GROUP)
        first[o] = start * GROUP

        @pl.when(here > 0)
        def _():
            lists[0, 64 + start] = 0

        start = start + here
        lists[1, 64 + o] = jnp.where(here > 0, start, 0)

    def place(s, carry):
        o = out_idx[s]

        @pl.when(o < OUTS)
        def _():
            p = first[o]
            q = lax.div(p, GROUP)
            g = p - q * GROUP
            lists[g, q] = s
            lists[GROUP + g, q] = amp_idx[s]
            first[o] = p + 1

        return carry

    lax.fori_loop(0, SLOTS, place, 0, unroll=2)


def slot_lists(out_idx, amp_idx):
    return pl.pallas_call(
        list_kernel,
        out_shape=jax.ShapeDtypeStruct((8, 128), jnp.int32),
        in_specs=[pl.BlockSpec(memory_space=pltpu.SMEM)] * 2,
        out_specs=pl.BlockSpec(memory_space=pltpu.SMEM),
        scratch_shapes=[pltpu.SMEM((8,), jnp.int32), pltpu.SMEM((8,), jnp.int32)],
        name="slot_lists",
    )(out_idx, amp_idx)


def ladder_kernel(lists, lists_hbm, amps, tiles, owned, *scratch):
    slices = scratch[:SUBS]
    gathered = [ref.reshape(4, 2, 4, 4, ROWS, LANES) for ref in slices]
    (tiles_own, tiles_sib, history, part, got1, sum1, got2, cross_out, cross_in, lists_in, lists_sib,
     send0, recv0, local0, send_ag, recv_ag, send1, recv1, send2, recv2, send_x, recv_x, misc) = scratch[SUBS:]
    row, col = lax.axis_index("row"), lax.axis_index("col")
    y, core = lax.div(row, 2), lax.rem(row, 2)
    z, x = lax.div(col, RING), lax.rem(col, RING)
    at = (y, z, x)
    sib = (y * 2 + 1 - core, col)

    def turn(value, by):
        return lax.rem(value + by + RING, RING)

    def peer(axis, by):
        place = list(at)
        place[axis] = turn(at[axis], by)
        return (place[Y] * 2 + core, place[Z] * RING + place[X])

    partners = [peer(a, d) for a in (Y, Z, X) for d in (1, -1)] + [peer(Z, 2), peer(X, 2), sib]
    barrier = pltpu.get_barrier_semaphore()
    for partner in partners:
        pl.semaphore_signal(barrier, inc=1, device_id=partner, device_id_type=MESH)
    pl.semaphore_wait(barrier, len(partners))

    sent = []

    def send(src, dst, s_sem, r_sem, to):
        copy = pltpu.make_async_remote_copy(
            src_ref=src, dst_ref=dst, send_sem=s_sem, recv_sem=r_sem, device_id=to, device_id_type=MESH
        )
        copy.start()
        sent.append(copy)

    def arrive(dst, s_sem, r_sem, to):
        pltpu.make_async_remote_copy(
            src_ref=dst, dst_ref=dst, send_sem=s_sem, recv_sem=r_sem, device_id=to, device_id_type=MESH
        ).wait_recv()

    here = []
    for s in range(SUBS):
        mine = pl.ds(pl.multiple_of(core * (SUBS * LANES) + s * LANES, LANES), LANES)
        other = pl.ds(pl.multiple_of((1 - core) * (SUBS * LANES) + s * LANES, LANES), LANES)
        home = gathered[s].at[y, core, z, x]
        send(amps.at[:, other], home, send0.at[s], recv0.at[s], sib)
        copy = pltpu.make_async_copy(amps.at[:, mine], home, local0.at[s])
        copy.start()
        here.append(copy)
    send(lists_hbm, lists_in, misc.at[0], misc.at[1], sib)
    send(tiles, tiles_sib.at[pl.ds(0, SLOTS)], misc.at[2], misc.at[3], sib)
    own_tiles = pltpu.make_async_copy(tiles, tiles_own.at[pl.ds(0, SLOTS)], misc.at[4])
    own_tiles.start()
    for ref in (tiles_own, tiles_sib):
        ref[SLOTS] = jnp.zeros((TILE, TILE), ref.dtype)
    history[0] = jnp.zeros((TILE, WIDE), jnp.float32)

    def region(s, phase, index, half):
        axis = ORDERS[s][phase]
        done = ORDERS[s][:phase]
        pick = [slice(None) if a in done else at[a] for a in (Y, Z, X)]
        pick[axis] = index
        return gathered[s].at[pick[Y], half, pick[Z], pick[X]]

    def spread(s, phase):
        axis = ORDERS[s][phase]
        mine = region(s, phase, at[axis], slice(None))
        for way, by in enumerate((1, -1)):
            n = phase * 4 + way
            send(mine, mine, send_ag.at[s, n], recv_ag.at[s, n], peer(axis, by))

    def forward(s, phase):
        axis = ORDERS[s][phase]
        for way, by in enumerate((1, -1)):
            n = phase * 4 + way
            index = turn(at[axis], -by)
            arrive(region(s, phase, index, slice(None)), send_ag.at[s, n], recv_ag.at[s, n], peer(axis, by))
            passed = region(s, phase, index, way)
            send(passed, passed, send_ag.at[s, n + 2], recv_ag.at[s, n + 2], peer(axis, by))

    def finish(s, phase):
        axis = ORDERS[s][phase]
        for way, by in enumerate((1, -1)):
            n = phase * 4 + 2 + way
            arrive(region(s, phase, turn(at[axis], 2), way), send_ag.at[s, n], recv_ag.at[s, n], peer(axis, by))

    for s in range(SUBS):
        here[s].wait()
        arrive(gathered[s].at[y, 1 - core, z, x], send0.at[s], recv0.at[s], sib)
        spread(s, 0)
    for phase in (0, 1):
        for s in range(SUBS):
            forward(s, phase)
        for s in range(SUBS):
            finish(s, phase)
            spread(s, phase + 1)

    own_tiles.wait()
    arrive(tiles_sib.at[pl.ds(0, SLOTS)], misc.at[2], misc.at[3], sib)
    arrive(lists_in, misc.at[0], misc.at[1], sib)
    to_scalar = pltpu.make_async_copy(lists_in, lists_sib, misc.at[5])
    to_scalar.start()
    to_scalar.wait()

    def products(k, group):
        which, tile_ref = ((lists, tiles_own), (lists_sib, tiles_sib))[group]
        per = SUBS // CHUNKS
        parts = slices[k * per : (k + 1) * per]

        def step(q, carry):
            left, right = [], []
            for g in range(GROUP):
                left.append(tile_ref[which[g, q]])
                m = which[GROUP + g, q]
                right.append(jnp.concatenate([ref[m] for ref in parts], axis=1))
            new = jnp.dot(
                jnp.concatenate(left, axis=1), jnp.concatenate(right, axis=0), preferred_element_type=jnp.float32
            )
            history[q + 1] = history[which[0, 64 + q]] + new
            return carry

        lax.fori_loop(0, QUADS, step, 0, unroll=2)
        rows_ref = part.at[k, group].reshape(OUTS * TILE, WIDE)
        for o in range(OUTS):
            rows_ref[o * TILE : (o + 1) * TILE, :] = history[which[1, 64 + o]]

    def pick_axis(ref, axis, index):
        return ref.at[:, :, index] if axis == Z else ref.at[:, :, :, index]

    steps = (1, -1, 2)

    def sum_send1(k):
        axis = SUM_ORDERS[k][0]
        for n, by in enumerate(steps):
            src = pick_axis(part.at[k], axis, turn(at[axis], by))
            send(src, got1.at[k, n], send1.at[k, n], recv1.at[k, n], peer(axis, by))

    def sum_step2(k):
        axis, then = SUM_ORDERS[k]
        for n, by in enumerate(steps):
            arrive(got1.at[k, n], send1.at[k, n], recv1.at[k, n], peer(axis, by))
        for g in range(2):
            for b in range(NB):
                for i in range(RING):
                    own = part[k, g, b, at[Z], i] if axis == Z else part[k, g, b, i, at[X]]
                    sum1[k, g, b, i] = (own + got1[k, 0, g, b, i]) + (got1[k, 1, g, b, i] + got1[k, 2, g, b, i])
        for n, by in enumerate(steps):
            src = sum1.at[k, :, :, turn(at[then], by)]
            send(src, got2.at[k, n], send2.at[k, n], recv2.at[k, n], peer(then, by))

    def sum_step3(k):
        then = SUM_ORDERS[k][1]
        for n, by in enumerate(steps):
            arrive(got2.at[k, n], send2.at[k, n], recv2.at[k, n], peer(then, by))
        for g in (1, 0):
            for b in range(NB):
                total = (sum1[k, g, b, at[then]] + got2[k, 0, g, b]) + (got2[k, 1, g, b] + got2[k, 2, g, b])
                if g == 1:
                    cross_out[k, b] = total
                else:
                    columns = pl.ds(pl.multiple_of(core * (SUBS * LANES) + k * WIDE, WIDE), WIDE)
                    owned[b, :, columns] = total
            if g == 1:
                send(cross_out.at[k], cross_in.at[k], send_x.at[k], recv_x.at[k], sib)

    def sum_step4(k):
        arrive(cross_in.at[k], send_x.at[k], recv_x.at[k], sib)
        for b in range(NB):
            columns = pl.ds(pl.multiple_of((1 - core) * (SUBS * LANES) + k * WIDE, WIDE), WIDE)
            owned[b, :, columns] = cross_in[k, b]

    per = SUBS // CHUNKS
    for s in range(per):
        forward(s, 2)
    for k in range(CHUNKS):
        for s in range(k * per, (k + 1) * per):
            finish(s, 2)
        products(k, 0)
        if k + 1 < CHUNKS:
            for s in range((k + 1) * per, (k + 2) * per):
                forward(s, 2)
        if k >= 1:
            sum_step2(k - 1)
        products(k, 1)
        sum_send1(k)
        if k >= 1:
            sum_step3(k - 1)
    sum_step2(CHUNKS - 1)
    sum_step3(CHUNKS - 1)
    for k in range(CHUNKS):
        sum_step4(k)
    for copy in sent:
        copy.wait_send()


def owned_ladder(lists, amplitudes, tiles):
    dma = pltpu.SemaphoreType.DMA
    vmem = pltpu.VMEM
    f32 = jnp.float32
    scratch = [vmem((2 * NT, TILE, LANES), jnp.bfloat16) for _ in range(SUBS)]
    scratch += [
        vmem((SLOTS + 1, TILE, TILE), jnp.bfloat16),
        vmem((SLOTS + 1, TILE, TILE), jnp.bfloat16),
        vmem((QUADS + 1, TILE, WIDE), f32),
        vmem((CHUNKS, 2, NB, RING, RING, OWN, WIDE), f32),
        vmem((CHUNKS, 3, 2, NB, RING, OWN, WIDE), f32),
        vmem((CHUNKS, 2, NB, RING, OWN, WIDE), f32),
        vmem((CHUNKS, 3, 2, NB, OWN, WIDE), f32),
        vmem((CHUNKS, NB, OWN, WIDE), f32),
        vmem((CHUNKS, NB, OWN, WIDE), f32),
        vmem((8, 128), jnp.int32),
        pltpu.SMEM((8, 128), jnp.int32),
        dma((SUBS,)), dma((SUBS,)), dma((SUBS,)),
        dma((SUBS, 12)), dma((SUBS, 12)),
        dma((CHUNKS, 3)), dma((CHUNKS, 3)), dma((CHUNKS, 3)), dma((CHUNKS, 3)),
        dma((CHUNKS,)), dma((CHUNKS,)), dma((6,)),
    ]
    return pl.pallas_call(
        ladder_kernel,
        out_shape=jax.ShapeDtypeStruct((NB, OWN, 2 * SUBS * LANES), f32),
        in_specs=[
            pl.BlockSpec(memory_space=pltpu.SMEM),
            pl.BlockSpec(memory_space=pl.ANY),
            pl.BlockSpec(memory_space=pl.ANY),
            pl.BlockSpec(memory_space=pl.ANY),
        ],
        out_specs=pl.BlockSpec(memory_space=pltpu.VMEM),
        scratch_shapes=scratch,
        compiler_params=pltpu.CompilerParams(
            collective_id=0, has_side_effects=True, vmem_limit_bytes=60 * 1024 * 1024
        ),
        name="ladder",
    )(lists, lists, amplitudes, tiles)


def per_device(amplitudes, integrals, slot_index, virt_energy, b_energy, pair_energy):
    index = slot_index.reshape(-1, 2)
    tiles = integrals.reshape(-1, TILE, TILE)
    lists = slot_lists(index[:, 0], index[:, 1])
    owned = owned_ladder(lists, amplitudes, tiles)
    denom = virt_energy[None, :, None] + b_energy[:, None, None] - pair_energy[None, None, :]
    return owned / denom


def solution(mesh):
    placed = (
        P(("row", "col"), None),
        P(("row", "col"), None, None, None, None),
        P(("row", "col"), None, None, None),
        P(("row", "col")),
        P(),
        P(),
    )
    return jax.shard_map(
        per_device,
        mesh=mesh,
        in_specs=placed,
        out_specs=P(None, ("row", "col"), None),
        check_vma=False,
    )
```

time: 1420 us -> 178 us (0.13)
  waiting for transfers between devices: 1060 us -> 0 us
  Pallas kernels: 0 us -> 172 us
  loops' own time: 160 us -> 0 us
  local copies, waits for them, and re-layouts: 78.7 us -> 1.46 us
  matrix products: 75.8 us -> 0 us
  blocking collectives: 14.7 us -> 0 us
    reduce_scatter x1 -> x0, waiting for transfers between devices: 940 us -> none  [per_device(): lax.psum_scatter(ladder_rows, 'col', scatter_dimension=1, tiled=True)]
    pallas_call x0 -> x2, Pallas kernels: none -> 172 us  [the longest x1 169 us: owned_ladder(): pl.pallas_call(ladder_kernel, out_shape=jax.ShapeDtypeStruct((NB, OWN, 2...]
    another operation x17 -> x0, loops' own time: 160 us -> none  [the longest x16 160 us: per_member(): return lax.fori_loop(0, filled[member], per_slot, partial_value)]
    dot_general x32 -> x0, matrix products: 75.8 us -> none  [per_slot(): contrib = jnp.dot(tile_now, operand, preferred_element_type=jnp.float32)]
    dynamic_slice x80 -> x0, local copies, waits for them, and re-layouts: 73.7 us -> none  [the longest x32 41.6 us: per_slot(): current = lax.dynamic_index_in_dim(acc, out_block, 0, keepdims=False)]
    all_to_all x1 -> x0, waiting for transfers between devices: 67.5 us -> none  [per_device(): lax.all_to_all(integrals, 'col', split_axis=1, concat_axis=1, tiled=True)]
    all_gather x1 -> x0, waiting for transfers between devices: 49.2 us -> none  [per_device(): whole = lax.all_gather(amplitudes, ('row', 'col'), axis=0, tiled=True)]
    all_to_all x1 -> x0, blocking collectives: 14.7 us -> none  [per_device(): lax.all_to_all(slot_index, 'col', split_axis=1, concat_axis=1, tiled=True)]
  transfers between devices with their start and end apart: 3 -> 0, of which waited for: 3 -> 0; matrix products, arithmetic and copies ran while one was open for 0% -> 0% of each run, Pallas kernels for 0% -> 0%
where the time goes in v2:
time: 178 us; the launch traced here: 176 us
  Pallas kernels  172 us (97%)
  other arithmetic  1.94 us (1%)
    pallas_call x1, Pallas kernels, owned_ladder(): pl.pallas_call(ladder_kernel, out_shape=jax.ShapeDtypeStruct((NB, OWN, 2...  169 us
    pallas_call x1, Pallas kernels, slot_lists(): pl.pallas_call(list_kernel, out_shape=jax.ShapeDtypeStruct((8, 128), jnp....  3.82 us

profile of v2, /device:TPU:1, one launch (start us, length us, event | category | flops | bytes accessed | tf_op | source)
XLA Modules:
  0.0 175.9 jit_solution(2812237485768334973)
XLA Ops:
  0.0 0.0 copy-start.2
  0.0 0.0 copy-start.1
  0.0 0.0 copy-start
  0.0 0.8 copy.7
  0.8 0.1 reshape.39
  0.9 0.6 slice_bitcast_fusion
  1.5 3.8 %slot_lists.1.lists.lists_hbm = s32[8,128]{1,0:T(8,128)} custom-call(s32[128]{0:T(128)} %get-tuple-element.6.out_idx, s32[128]{0:T(128)} %get-tuple-element.5.amp_idx), custom_call_target="tpu_custom_call" | custom-call | tf_op jit(solution)/shard_map/slot_lists/pallas_call | solution.py:84
  5.3 168.6 %ladder.1 = f32[2,24,2048]{2,1,0:T(8,128)} custom-call(s32[8,128]{1,0:T(8,128)} %slot_lists.1.lists.lists_hbm, s32[8,128]{1,0:T(8,128)} %slot_lists.1.lists.lists_hbm, bf16[48,2048]{1,0:T(8,128)(2,1)} %amps.1, bf16[128,128,128]{2,1,0:T(8,128)(2,1)} %bitcast.9), custom_call_target="tpu_custom_call" | custom-call | tf_op jit(solution)/shard_map/ladder/pallas_call | solution.py:310
  173.9 0.0 copy-done.2
  173.9 0.0 copy-done.1
  173.9 0.1 broadcast_add_fusion
  174.0 0.0 copy-done
  174.0 1.9 %subtract_divide_fusion = f32[2,24,2048]{2,1,0:T(8,128)} fusion(f32[2,24,2048]{2,1,0:T(8,128)} %ladder.1, f32[2048]{0:T(1024)S(1)} %copy-done, f32[2,24]{1,0:T(2,128)S(1)} %broadcast_add_fusion), kind=kLoop, calls=%fused_computation | loop fusion | flops 196608 | bytes 794816 | tf_op jit(solution)/shard_map/div | solution.py:334
Async XLA Ops:
  0.0 173.9 %copy-start.2 = (f32[2]{0:T(128)S(1)}, f32[2]{0:T(128)}, u32[]{:S(2)}) copy-start(f32[2]{0:T(128)} %param.10) | copy-start | bytes 28
  0.0 173.9 %copy-start.1 = (f32[24]{0:T(128)S(1)}, f32[24]{0:T(128)}, u32[]{:S(2)}) copy-start(f32[24]{0:T(128)} %param.9) | copy-start | bytes 292
  0.0 174.0 %copy-start = (f32[2048]{0:T(1024)S(1)}, f32[2048]{0:T(1024)}, u32[]{:S(2)}) copy-start(f32[2048]{0:T(1024)} %param.11) | copy-start | bytes 24580

commit v3 on v2

--- a/solution.py
+++ b/solution.py
@@ -24,12 +24,12 @@
 RING = 4
 Y, Z, X = 0, 1, 2
 ORDERS = (
-    (X, Z, Y), (Y, Z, X),
-    (Z, X, Y), (Y, X, Z),
-    (X, Z, Y), (Y, Z, X),
-    (Z, X, Y), (Y, X, Z),
+    (X, Z, Y), (Z, Y, X),
+    (Z, X, Y), (X, Y, Z),
+    (Z, Y, X), (X, Y, Z),
+    (X, Z, Y), (Z, X, Y),
 )
-SUM_ORDERS = ((X, Z), (Z, X), (X, Z), (Z, X))
+SUM_ORDERS = ((X, Z), (Z, X))
 
 
 def list_kernel(out_idx, amp_idx, lists, fill, first):
@@ -94,7 +94,7 @@
 def ladder_kernel(lists, lists_hbm, amps, tiles, owned, *scratch):
     slices = scratch[:SUBS]
     gathered = [ref.reshape(4, 2, 4, 4, ROWS, LANES) for ref in slices]
-    (tiles_own, tiles_sib, history, part, got1, sum1, got2, cross_out, cross_in, lists_in, lists_sib,
+    (tiles_own, tiles_sib, history, part, relay, got1, sum1, got2, cross_out, cross_in, lists_in, lists_sib,
      send0, recv0, local0, send_ag, recv_ag, send1, recv1, send2, recv2, send_x, recv_x, misc) = scratch[SUBS:]
     row, col = lax.axis_index("row"), lax.axis_index("col")
     y, core = lax.div(row, 2), lax.rem(row, 2)
@@ -110,7 +110,7 @@
         place[axis] = turn(at[axis], by)
         return (place[Y] * 2 + core, place[Z] * RING + place[X])
 
-    partners = [peer(a, d) for a in (Y, Z, X) for d in (1, -1)] + [peer(Z, 2), peer(X, 2), sib]
+    partners = [peer(a, d) for a in (Y, Z, X) for d in (1, -1)] + [peer(a, 2) for a in (Y, Z, X)] + [sib]
     barrier = pltpu.get_barrier_semaphore()
     for partner in partners:
         pl.semaphore_signal(barrier, inc=1, device_id=partner, device_id_type=MESH)
@@ -154,45 +154,67 @@
         pick[axis] = index
         return gathered[s].at[pick[Y], half, pick[Z], pick[X]]
 
+    steps = (1, -1, 2)
+
     def spread(s, phase):
         axis = ORDERS[s][phase]
         mine = region(s, phase, at[axis], slice(None))
-        for way, by in enumerate((1, -1)):
-            n = phase * 4 + way
-            send(mine, mine, send_ag.at[s, n], recv_ag.at[s, n], peer(axis, by))
-
-    def forward(s, phase):
-        axis = ORDERS[s][phase]
-        for way, by in enumerate((1, -1)):
-            n = phase * 4 + way
-            index = turn(at[axis], -by)
-            arrive(region(s, phase, index, slice(None)), send_ag.at[s, n], recv_ag.at[s, n], peer(axis, by))
-            passed = region(s, phase, index, way)
-            send(passed, passed, send_ag.at[s, n + 2], recv_ag.at[s, n + 2], peer(axis, by))
+        for n, by in enumerate(steps):
+            send(mine, mine, send_ag.at[s, phase * 3 + n], recv_ag.at[s, phase * 3 + n], peer(axis, by))
 
     def finish(s, phase):
         axis = ORDERS[s][phase]
-        for way, by in enumerate((1, -1)):
-            n = phase * 4 + 2 + way
-            arrive(region(s, phase, turn(at[axis], 2), way), send_ag.at[s, n], recv_ag.at[s, n], peer(axis, by))
-
-    for s in range(SUBS):
+        for n, by in enumerate(steps):
+            ref = region(s, phase, turn(at[axis], -by), slice(None))
+            arrive(ref, send_ag.at[s, phase * 3 + n], recv_ag.at[s, phase * 3 + n], peer(axis, by))
+
+    def last_spread(s):
+        axis = ORDERS[s][2]
+        for turn_of in range(2):
+            for way, by in enumerate((1, -1)):
+                n = 6 + way * 2 + turn_of
+                mine = region(s, 2, at[axis], way ^ turn_of)
+                send(mine, mine, send_ag.at[s, n], recv_ag.at[s, n], peer(axis, by))
+
+    def last_forward(s):
+        axis = ORDERS[s][2]
+        for way, by in enumerate((1, -1)):
+            n = 6 + way * 2
+            passed = region(s, 2, turn(at[axis], -by), way)
+            arrive(passed, send_ag.at[s, n], recv_ag.at[s, n], peer(axis, by))
+            send(passed, passed, send_ag.at[s, 10 + way], recv_ag.at[s, 10 + way], peer(axis, by))
+
+    def last_rest(s):
+        axis = ORDERS[s][2]
+        for way, by in enumerate((1, -1)):
+            n = 7 + way * 2
+            arrive(region(s, 2, turn(at[axis], -by), 1 - way), send_ag.at[s, n], recv_ag.at[s, n], peer(axis, by))
+
+    def last_finish(s):
+        axis = ORDERS[s][2]
+        for way, by in enumerate((1, -1)):
+            arrive(region(s, 2, turn(at[axis], 2), way), send_ag.at[s, 10 + way], recv_ag.at[s, 10 + way], peer(axis, by))
+
+    def first(s):
         here[s].wait()
         arrive(gathered[s].at[y, 1 - core, z, x], send0.at[s], recv0.at[s], sib)
         spread(s, 0)
-    for phase in (0, 1):
-        for s in range(SUBS):
-            forward(s, phase)
-        for s in range(SUBS):
-            finish(s, phase)
-            spread(s, phase + 1)
-
-    own_tiles.wait()
-    arrive(tiles_sib.at[pl.ds(0, SLOTS)], misc.at[2], misc.at[3], sib)
-    arrive(lists_in, misc.at[0], misc.at[1], sib)
-    to_scalar = pltpu.make_async_copy(lists_in, lists_sib, misc.at[5])
-    to_scalar.start()
-    to_scalar.wait()
+
+    def second(s):
+        finish(s, 0)
+        spread(s, 1)
+
+    def third(s):
+        finish(s, 1)
+        last_spread(s)
+
+    def slots_ready(_):
+        own_tiles.wait()
+        arrive(tiles_sib.at[pl.ds(0, SLOTS)], misc.at[2], misc.at[3], sib)
+        arrive(lists_in, misc.at[0], misc.at[1], sib)
+        to_scalar = pltpu.make_async_copy(lists_in, lists_sib, misc.at[5])
+        to_scalar.start()
+        to_scalar.wait()
 
     def products(k, group):
         which, tile_ref = ((lists, tiles_own), (lists_sib, tiles_sib))[group]
@@ -211,76 +233,87 @@
             history[q + 1] = history[which[0, 64 + q]] + new
             return carry
 
-        lax.fori_loop(0, QUADS, step, 0, unroll=2)
+        lax.fori_loop(0, QUADS, step, 0, unroll=6)
         rows_ref = part.at[k, group].reshape(OUTS * TILE, WIDE)
         for o in range(OUTS):
             rows_ref[o * TILE : (o + 1) * TILE, :] = history[which[1, 64 + o]]
 
-    def pick_axis(ref, axis, index):
-        return ref.at[:, :, index] if axis == Z else ref.at[:, :, :, index]
-
-    steps = (1, -1, 2)
-
-    def sum_send1(k):
-        axis = SUM_ORDERS[k][0]
+    def block(k, g, b, axis, index):
+        return part.at[k, g, b, index] if axis == Z else part.at[k, g, b, :, index]
+
+    def sum_send(k, g):
+        axis = SUM_ORDERS[g][0]
+        for way, by in enumerate((1, -1)):
+            far = block(k, g, way, axis, turn(at[axis], 2))
+            send(far, relay.at[k, g, way], send1.at[k, g, way], recv1.at[k, g, way], peer(axis, by))
+        for way, by in enumerate((1, -1)):
+            near = block(k, g, 1 - way, axis, turn(at[axis], by))
+            send(near, got1.at[k, g, way, 1 - way], send1.at[k, g, 2 + way], recv1.at[k, g, 2 + way], peer(axis, by))
+
+    def sum_relay(k, g):
+        axis = SUM_ORDERS[g][0]
+        for way, by in enumerate((1, -1)):
+            arrive(relay.at[k, g, way], send1.at[k, g, way], recv1.at[k, g, way], peer(axis, by))
+            index = turn(at[axis], by)
+            for i in range(RING):
+                own = part[k, g, way, index, i] if axis == Z else part[k, g, way, i, index]
+                relay[k, g, way, i] = relay[k, g, way, i] + own
+            send(relay.at[k, g, way], got1.at[k, g, way, way], send1.at[k, g, 4 + way], recv1.at[k, g, 4 + way], peer(axis, by))
+
+    def sum_pass(k, g):
+        axis, then = SUM_ORDERS[g]
+        for way, by in enumerate((1, -1)):
+            for n, b in ((2, 1 - way), (4, way)):
+                arrive(got1.at[k, g, way, b], send1.at[k, g, n + way], recv1.at[k, g, n + way], peer(axis, by))
+        for b in range(NB):
+            for i in range(RING):
+                own = part[k, g, b, at[Z], i] if axis == Z else part[k, g, b, i, at[X]]
+                sum1[k, g, b, i] = own + (got1[k, g, 0, b, i] + got1[k, g, 1, b, i])
         for n, by in enumerate(steps):
-            src = pick_axis(part.at[k], axis, turn(at[axis], by))
-            send(src, got1.at[k, n], send1.at[k, n], recv1.at[k, n], peer(axis, by))
-
-    def sum_step2(k):
-        axis, then = SUM_ORDERS[k]
+            src = sum1.at[k, g, :, turn(at[then], by)]
+            send(src, got2.at[k, g, n], send2.at[k, g, n], recv2.at[k, g, n], peer(then, by))
+
+    def sum_end(k, g):
+        then = SUM_ORDERS[g][1]
         for n, by in enumerate(steps):
-            arrive(got1.at[k, n], send1.at[k, n], recv1.at[k, n], peer(axis, by))
-        for g in range(2):
-            for b in range(NB):
-                for i in range(RING):
-                    own = part[k, g, b, at[Z], i] if axis == Z else part[k, g, b, i, at[X]]
-                    sum1[k, g, b, i] = (own + got1[k, 0, g, b, i]) + (got1[k, 1, g, b, i] + got1[k, 2, g, b, i])
-        for n, by in enumerate(steps):
-            src = sum1.at[k, :, :, turn(at[then], by)]
-            send(src, got2.at[k, n], send2.at[k, n], recv2.at[k, n], peer(then, by))
-
-    def sum_step3(k):
-        then = SUM_ORDERS[k][1]
-        for n, by in enumerate(steps):
-            arrive(got2.at[k, n], send2.at[k, n], recv2.at[k, n], peer(then, by))
-        for g in (1, 0):
-            for b in range(NB):
-                total = (sum1[k, g, b, at[then]] + got2[k, 0, g, b]) + (got2[k, 1, g, b] + got2[k, 2, g, b])
-                if g == 1:
-                    cross_out[k, b] = total
-                else:
-                    columns = pl.ds(pl.multiple_of(core * (SUBS * LANES) + k * WIDE, WIDE), WIDE)
-                    owned[b, :, columns] = total
+            arrive(got2.at[k, g, n], send2.at[k, g, n], recv2.at[k, g, n], peer(then, by))
+        for b in range(NB):
+            total = (sum1[k, g, b, at[then]] + got2[k, g, 0, b]) + (got2[k, g, 1, b] + got2[k, g, 2, b])
             if g == 1:
-                send(cross_out.at[k], cross_in.at[k], send_x.at[k], recv_x.at[k], sib)
-
-    def sum_step4(k):
+                cross_out[k, b] = total
+            else:
+                columns = pl.ds(pl.multiple_of(core * (SUBS * LANES) + k * WIDE, WIDE), WIDE)
+                owned[b, :, columns] = total
+        if g == 1:
+            send(cross_out.at[k], cross_in.at[k], send_x.at[k], recv_x.at[k], sib)
+
+    def sum_cross(k):
         arrive(cross_in.at[k], send_x.at[k], recv_x.at[k], sib)
         for b in range(NB):
             columns = pl.ds(pl.multiple_of((1 - core) * (SUBS * LANES) + k * WIDE, WIDE), WIDE)
             owned[b, :, columns] = cross_in[k, b]
 
-    per = SUBS // CHUNKS
-    for s in range(per):
-        forward(s, 2)
+    def unit(work):
+        return lambda n: work(n // 2, n % 2)
+
+    fwd, rest, done = last_forward, last_rest, last_finish
+    mul, out, mid, add, end = (unit(w) for w in (products, sum_send, sum_relay, sum_pass, sum_end))
+    plan = [(first, s) for s in range(SUBS)]
+    plan += [(second, s) for s in (0, 1, 3, 2)] + [(third, s) for s in (0, 1, 3)]
+    plan += [(second, s) for s in (4, 5, 6, 7)] + [(slots_ready, 0)]
+    plan += [(fwd, 0), (fwd, 1), (fwd, 3), (rest, 0), (third, 2), (rest, 1), (third, 4), (rest, 3), (third, 5)]
+    plan += [(done, 0), (done, 1), (mul, 0), (out, 0)]
+    plan += [(fwd, 2), (mul, 1), (out, 1), (mid, 0)]
+    plan += [(rest, 2), (third, 6), (fwd, 4), (fwd, 5), (done, 2), (done, 3), (mul, 2), (out, 2), (mid, 1), (add, 0)]
+    plan += [(third, 7), (mul, 3), (out, 3), (mid, 2), (add, 1), (fwd, 6)]
+    plan += [(rest, 4), (rest, 5), (done, 4), (done, 5), (mul, 4), (out, 4), (mid, 3), (add, 2), (end, 0), (fwd, 7)]
+    plan += [(mul, 5), (out, 5), (mid, 4), (add, 3), (end, 1)]
+    plan += [(rest, 6), (rest, 7), (done, 6), (done, 7), (mul, 6), (out, 6), (mid, 5), (add, 4), (end, 2)]
+    plan += [(mul, 7), (out, 7), (mid, 6), (add, 5), (end, 3), (mid, 7), (add, 6), (end, 4), (end, 5), (add, 7), (end, 6), (end, 7)]
+    for work, which in plan:
+        work(which)
     for k in range(CHUNKS):
-        for s in range(k * per, (k + 1) * per):
-            finish(s, 2)
-        products(k, 0)
-        if k + 1 < CHUNKS:
-            for s in range((k + 1) * per, (k + 2) * per):
-                forward(s, 2)
-        if k >= 1:
-            sum_step2(k - 1)
-        products(k, 1)
-        sum_send1(k)
-        if k >= 1:
-            sum_step3(k - 1)
-    sum_step2(CHUNKS - 1)
-    sum_step3(CHUNKS - 1)
-    for k in range(CHUNKS):
-        sum_step4(k)
+        sum_cross(k)
     for copy in sent:
         copy.wait_send()
 
@@ -295,16 +328,17 @@
         vmem((SLOTS + 1, TILE, TILE), jnp.bfloat16),
         vmem((QUADS + 1, TILE, WIDE), f32),
         vmem((CHUNKS, 2, NB, RING, RING, OWN, WIDE), f32),
-        vmem((CHUNKS, 3, 2, NB, RING, OWN, WIDE), f32),
+        vmem((CHUNKS, 2, 2, RING, OWN, WIDE), f32),
+        vmem((CHUNKS, 2, 2, NB, RING, OWN, WIDE), f32),
         vmem((CHUNKS, 2, NB, RING, OWN, WIDE), f32),
-        vmem((CHUNKS, 3, 2, NB, OWN, WIDE), f32),
+        vmem((CHUNKS, 2, 3, NB, OWN, WIDE), f32),
         vmem((CHUNKS, NB, OWN, WIDE), f32),
         vmem((CHUNKS, NB, OWN, WIDE), f32),
         vmem((8, 128), jnp.int32),
         pltpu.SMEM((8, 128), jnp.int32),
         dma((SUBS,)), dma((SUBS,)), dma((SUBS,)),
         dma((SUBS, 12)), dma((SUBS, 12)),
-        dma((CHUNKS, 3)), dma((CHUNKS, 3)), dma((CHUNKS, 3)), dma((CHUNKS, 3)),
+        dma((CHUNKS, 2, 6)), dma((CHUNKS, 2, 6)), dma((CHUNKS, 2, 3)), dma((CHUNKS, 2, 3)),
         dma((CHUNKS,)), dma((CHUNKS,)), dma((6,)),
     ]
     return pl.pallas_call(

time: 178 us -> 118 us (0.66); the launches traced: 176 us -> 118 us
  Pallas kernels: 172 us -> 114 us
    pallas_call x1, Pallas kernels: 169 us -> 110 us  [owned_ladder(): pl.pallas_call(ladder_kernel, out_shape=jax.ShapeDtypeStruct((NB, OWN, 2...]
where the time goes in v3:
time: 118 us
  Pallas kernels  114 us (97%)
  other arithmetic  1.94 us (2%)
  local copies, waits for them, and re-layouts  1.46 us (1%)
    pallas_call x1, Pallas kernels, owned_ladder(): pl.pallas_call(ladder_kernel, out_shape=jax.ShapeDtypeStruct((NB, OWN, 2...  110 us
    pallas_call x1, Pallas kernels, slot_lists(): pl.pallas_call(list_kernel, out_shape=jax.ShapeDtypeStruct((8, 128), jnp....  3.82 us

profile of v3, /device:TPU:1, one launch (start us, length us, event | category | flops | bytes accessed | tf_op | source)
XLA Modules:
  0.0 117.7 jit_solution(1880626643320314858)
XLA Ops:
  0.0 0.0 copy-start.2
  0.0 0.0 copy-start.1
  0.0 0.0 copy-start
  0.0 0.8 copy.7
  0.8 0.1 reshape.39
  0.9 0.6 slice_bitcast_fusion
  1.5 3.8 %slot_lists.1.lists.lists_hbm = s32[8,128]{1,0:T(8,128)} custom-call(s32[128]{0:T(128)} %get-tuple-element.6.out_idx, s32[128]{0:T(128)} %get-tuple-element.5.amp_idx), custom_call_target="tpu_custom_call" | custom-call | tf_op jit(solution)/shard_map/slot_lists/pallas_call | solution.py:84
  5.3 110.5 %ladder.1 = f32[2,24,2048]{2,1,0:T(8,128)} custom-call(s32[8,128]{1,0:T(8,128)} %slot_lists.1.lists.lists_hbm, s32[8,128]{1,0:T(8,128)} %slot_lists.1.lists.lists_hbm, bf16[48,2048]{1,0:T(8,128)(2,1)} %amps.1, bf16[128,128,128]{2,1,0:T(8,128)(2,1)} %bitcast.9), custom_call_target="tpu_custom_call" | custom-call | tf_op jit(solution)/shard_map/ladder/pallas_call | solution.py:344
  115.7 0.0 copy-done.2
  115.8 0.0 copy-done.1
  115.8 0.1 broadcast_add_fusion
  115.8 0.0 copy-done
  115.8 1.9 %subtract_divide_fusion = f32[2,24,2048]{2,1,0:T(8,128)} fusion(f32[2,24,2048]{2,1,0:T(8,128)} %ladder.1, f32[2048]{0:T(1024)S(1)} %copy-done, f32[2,24]{1,0:T(2,128)S(1)} %broadcast_add_fusion), kind=kLoop, calls=%fused_computation | loop fusion | flops 196608 | bytes 794816 | tf_op jit(solution)/shard_map/div | solution.py:368
Async XLA Ops:
  0.0 115.8 %copy-start.2 = (f32[2]{0:T(128)S(1)}, f32[2]{0:T(128)}, u32[]{:S(2)}) copy-start(f32[2]{0:T(128)} %param.10) | copy-start | bytes 28
  0.0 115.8 %copy-start.1 = (f32[24]{0:T(128)S(1)}, f32[24]{0:T(128)}, u32[]{:S(2)}) copy-start(f32[24]{0:T(128)} %param.9) | copy-start | bytes 292
  0.0 115.8 %copy-start = (f32[2048]{0:T(1024)S(1)}, f32[2048]{0:T(1024)}, u32[]{:S(2)}) copy-start(f32[2048]{0:T(1024)} %param.11) | copy-start | bytes 24580

commit v4 on v3

--- a/solution.py
+++ b/solution.py
@@ -26,75 +26,43 @@
 ORDERS = (
     (X, Z, Y), (Z, Y, X),
     (Z, X, Y), (X, Y, Z),
-    (Z, Y, X), (X, Y, Z),
+    (Y, Z, X), (Y, X, Z),
     (X, Z, Y), (Z, X, Y),
 )
 SUM_ORDERS = ((X, Z), (Z, X))
 
 
-def list_kernel(out_idx, amp_idx, lists, fill, first):
-    for o in range(OUTS + 1):
-        fill[o] = 0
-
-    def count(s, carry):
-        o = out_idx[s]
-        fill[o] = fill[o] + 1
-        return carry
-
-    lax.fori_loop(0, SLOTS, count, 0, unroll=4)
-
-    def blank(q, carry):
-        for g in range(GROUP):
-            lists[g, q] = SLOTS
-            lists[GROUP + g, q] = 0
-        lists[0, 64 + q] = q
-        return carry
-
-    lax.fori_loop(0, QUADS, blank, 0, unroll=2)
-    start = jnp.int32(0)
+def slot_lists(named):
+    i32 = jnp.int32
+    square = (SLOTS, SLOTS)
+    down, along = lax.broadcasted_iota(i32, square, 0), lax.broadcasted_iota(i32, square, 1)
+    out_along = jnp.broadcast_to(named[0:1, :], square)
+    out_down, amp_down = out_along.T, jnp.broadcast_to(named[1:2, :], square).T
+    same_before = jnp.where((out_along == out_down) & (along < down), 1, 0)
+    rank = jnp.sum(same_before, axis=1, keepdims=True)
+    start = jnp.zeros((1, SLOTS), i32)
+    place = jnp.full(square, -1, i32)
+    lane = along[0:1, :]
+    came_from, ends = lane, jnp.zeros((1, SLOTS), i32)
     for o in range(OUTS):
-        here = lax.div(fill[o] + (GROUP - 1), GROUP)
-        first[o] = start * GROUP
-
-        @pl.when(here > 0)
-        def _():
-            lists[0, 64 + start] = 0
-
-        start = start + here
-        lists[1, 64 + o] = jnp.where(here > 0, start, 0)
-
-    def place(s, carry):
-        o = out_idx[s]
-
-        @pl.when(o < OUTS)
-        def _():
-            p = first[o]
-            q = lax.div(p, GROUP)
-            g = p - q * GROUP
-            lists[g, q] = s
-            lists[GROUP + g, q] = amp_idx[s]
-            first[o] = p + 1
-
-        return carry
-
-    lax.fori_loop(0, SLOTS, place, 0, unroll=2)
-
-
-def slot_lists(out_idx, amp_idx):
-    return pl.pallas_call(
-        list_kernel,
-        out_shape=jax.ShapeDtypeStruct((8, 128), jnp.int32),
-        in_specs=[pl.BlockSpec(memory_space=pltpu.SMEM)] * 2,
-        out_specs=pl.BlockSpec(memory_space=pltpu.SMEM),
-        scratch_shapes=[pltpu.SMEM((8,), jnp.int32), pltpu.SMEM((8,), jnp.int32)],
-        name="slot_lists",
-    )(out_idx, amp_idx)
-
-
-def ladder_kernel(lists, lists_hbm, amps, tiles, owned, *scratch):
+        count = jnp.sum(jnp.where(out_down == o, 1, 0), axis=0, keepdims=True)
+        quads = (count + (GROUP - 1)) >> 2
+        place = jnp.where(out_down == o, start * GROUP + rank, place)
+        came_from = jnp.where((lane == start) & (count > 0), 0, came_from)
+        start = start + quads
+        ends = jnp.where((lane == o) & (count > 0), start, ends)
+    tiles, amps = [], []
+    for g in range(GROUP):
+        here = place == along * GROUP + g
+        tiles.append(SLOTS + jnp.sum(jnp.where(here, down - SLOTS, 0), axis=0, keepdims=True))
+        amps.append(jnp.sum(jnp.where(here, amp_down, 0), axis=0, keepdims=True))
+    return tiles + amps + [came_from, ends]
+
+
+def ladder_kernel(named, amps, tiles, owned, *scratch):
     slices = scratch[:SUBS]
     gathered = [ref.reshape(4, 2, 4, 4, ROWS, LANES) for ref in slices]
-    (tiles_own, tiles_sib, history, part, relay, got1, sum1, got2, cross_out, cross_in, lists_in, lists_sib,
+    (tiles_own, tiles_sib, history, part, relay, got1, sum1, got2, cross_out, cross_in, lists_out, lists_in, lists, lists_sib,
      send0, recv0, local0, send_ag, recv_ag, send1, recv1, send2, recv2, send_x, recv_x, misc) = scratch[SUBS:]
     row, col = lax.axis_index("row"), lax.axis_index("col")
     y, core = lax.div(row, 2), lax.rem(row, 2)
@@ -139,7 +107,6 @@
         copy = pltpu.make_async_copy(amps.at[:, mine], home, local0.at[s])
         copy.start()
         here.append(copy)
-    send(lists_hbm, lists_in, misc.at[0], misc.at[1], sib)
     send(tiles, tiles_sib.at[pl.ds(0, SLOTS)], misc.at[2], misc.at[3], sib)
     own_tiles = pltpu.make_async_copy(tiles, tiles_own.at[pl.ds(0, SLOTS)], misc.at[4])
     own_tiles.start()
@@ -207,6 +174,16 @@
     def third(s):
         finish(s, 1)
         last_spread(s)
+
+    def slots_sent(_):
+        for n, row_of in enumerate(slot_lists(named[...])):
+            lists_out[n : n + 1, :] = row_of
+        for n in range(10, 16):
+            lists_out[n : n + 1, :] = jnp.zeros((1, SLOTS), jnp.int32)
+        send(lists_out, lists_in, misc.at[0], misc.at[1], sib)
+        to_scalar = pltpu.make_async_copy(lists_out, lists, misc.at[6])
+        to_scalar.start()
+        to_scalar.wait()
 
     def slots_ready(_):
         own_tiles.wait()
@@ -230,13 +207,13 @@
             new = jnp.dot(
                 jnp.concatenate(left, axis=1), jnp.concatenate(right, axis=0), preferred_element_type=jnp.float32
             )
-            history[q + 1] = history[which[0, 64 + q]] + new
+            history[q + 1] = history[which[8, q]] + new
             return carry
 
-        lax.fori_loop(0, QUADS, step, 0, unroll=6)
+        lax.fori_loop(0, QUADS, step, 0, unroll=12)
         rows_ref = part.at[k, group].reshape(OUTS * TILE, WIDE)
         for o in range(OUTS):
-            rows_ref[o * TILE : (o + 1) * TILE, :] = history[which[1, 64 + o]]
+            rows_ref[o * TILE : (o + 1) * TILE, :] = history[which[9, o]]
 
     def block(k, g, b, axis, index):
         return part.at[k, g, b, index] if axis == Z else part.at[k, g, b, :, index]
@@ -298,9 +275,9 @@
 
     fwd, rest, done = last_forward, last_rest, last_finish
     mul, out, mid, add, end = (unit(w) for w in (products, sum_send, sum_relay, sum_pass, sum_end))
-    plan = [(first, s) for s in range(SUBS)]
-    plan += [(second, s) for s in (0, 1, 3, 2)] + [(third, s) for s in (0, 1, 3)]
-    plan += [(second, s) for s in (4, 5, 6, 7)] + [(slots_ready, 0)]
+    plan = [(first, s) for s in (0, 1, 3, 2)] + [(slots_sent, 0)] + [(second, s) for s in (0, 1, 3, 2)]
+    plan += [(first, s) for s in (4, 5, 6, 7)] + [(third, s) for s in (0, 1, 3)]
+    plan += [(second, s) for s in (6, 7, 4, 5)] + [(slots_ready, 0)]
     plan += [(fwd, 0), (fwd, 1), (fwd, 3), (rest, 0), (third, 2), (rest, 1), (third, 4), (rest, 3), (third, 5)]
     plan += [(done, 0), (done, 1), (mul, 0), (out, 0)]
     plan += [(fwd, 2), (mul, 1), (out, 1), (mid, 0)]
@@ -318,7 +295,7 @@
         copy.wait_send()
 
 
-def owned_ladder(lists, amplitudes, tiles):
+def owned_ladder(named, amplitudes, tiles):
     dma = pltpu.SemaphoreType.DMA
     vmem = pltpu.VMEM
     f32 = jnp.float32
@@ -334,19 +311,20 @@
         vmem((CHUNKS, 2, 3, NB, OWN, WIDE), f32),
         vmem((CHUNKS, NB, OWN, WIDE), f32),
         vmem((CHUNKS, NB, OWN, WIDE), f32),
-        vmem((8, 128), jnp.int32),
-        pltpu.SMEM((8, 128), jnp.int32),
+        vmem((16, 128), jnp.int32),
+        vmem((16, 128), jnp.int32),
+        pltpu.SMEM((16, 128), jnp.int32),
+        pltpu.SMEM((16, 128), jnp.int32),
         dma((SUBS,)), dma((SUBS,)), dma((SUBS,)),
         dma((SUBS, 12)), dma((SUBS, 12)),
         dma((CHUNKS, 2, 6)), dma((CHUNKS, 2, 6)), dma((CHUNKS, 2, 3)), dma((CHUNKS, 2, 3)),
-        dma((CHUNKS,)), dma((CHUNKS,)), dma((6,)),
+        dma((CHUNKS,)), dma((CHUNKS,)), dma((8,)),
     ]
     return pl.pallas_call(
         ladder_kernel,
         out_shape=jax.ShapeDtypeStruct((NB, OWN, 2 * SUBS * LANES), f32),
         in_specs=[
-            pl.BlockSpec(memory_space=pltpu.SMEM),
-            pl.BlockSpec(memory_space=pl.ANY),
+            pl.BlockSpec(memory_space=pltpu.VMEM),
             pl.BlockSpec(memory_space=pl.ANY),
             pl.BlockSpec(memory_space=pl.ANY),
         ],
@@ -356,14 +334,13 @@
             collective_id=0, has_side_effects=True, vmem_limit_bytes=60 * 1024 * 1024
         ),
         name="ladder",
-    )(lists, lists, amplitudes, tiles)
+    )(named, amplitudes, tiles)
 
 
 def per_device(amplitudes, integrals, slot_index, virt_energy, b_energy, pair_energy):
-    index = slot_index.reshape(-1, 2)
+    named = slot_index.reshape(-1, 2).T
     tiles = integrals.reshape(-1, TILE, TILE)
-    lists = slot_lists(index[:, 0], index[:, 1])
-    owned = owned_ladder(lists, amplitudes, tiles)
+    owned = owned_ladder(named, amplitudes, tiles)
     denom = virt_energy[None, :, None] + b_energy[:, None, None] - pair_energy[None, None, :]
     return owned / denom
 

time: 118 us -> 108 us (0.915)
  Pallas kernels: 114 us -> 104 us
    pallas_call x1, Pallas kernels: 110 us -> 104 us  [owned_ladder(): pl.pallas_call(ladder_kernel, out_shape=jax.ShapeDtypeStruct((NB, OWN, 2...]
    pallas_call x1 -> x0, Pallas kernels: 3.82 us -> none  [slot_lists(): pl.pallas_call(list_kernel, out_shape=jax.ShapeDtypeStruct((8, 128), jnp....]
where the time goes in v4:
time: 108 us
  Pallas kernels  104 us (96%)
  other arithmetic  1.94 us (2%)
  local copies, waits for them, and re-layouts  1.47 us (1%)
    pallas_call x1, Pallas kernels, owned_ladder(): pl.pallas_call(ladder_kernel, out_shape=jax.ShapeDtypeStruct((NB, OWN, 2...  104 us

profile of v4, /device:TPU:1, one launch (start us, length us, event | category | flops | bytes accessed | tf_op | source)
XLA Modules:
  0.0 107.9 jit_solution(10593103857354257686)
XLA Ops:
  0.0 0.0 copy-start.2
  0.0 0.0 copy-start.1
  0.0 0.0 copy-start
  0.0 0.8 copy.8
  0.8 0.7 reshape.39
  1.5 104.4 %ladder.1 = f32[2,24,2048]{2,1,0:T(8,128)} custom-call(s32[2,128]{1,0:T(2,128)} %bitcast.7, bf16[48,2048]{1,0:T(8,128)(2,1)} %amps.1, bf16[128,128,128]{2,1,0:T(8,128)(2,1)} %bitcast.6), custom_call_target="tpu_custom_call" | custom-call | tf_op jit(solution)/shard_map/ladder/pallas_call | solution.py:323
  105.9 0.0 copy-done.2
  105.9 0.0 copy-done.1
  105.9 0.1 broadcast_add_fusion
  106.0 0.0 copy-done
  106.0 1.9 %subtract_divide_fusion = f32[2,24,2048]{2,1,0:T(8,128)} fusion(f32[2,24,2048]{2,1,0:T(8,128)} %ladder.1, f32[2048]{0:T(1024)S(1)} %copy-done, f32[2,24]{1,0:T(2,128)S(1)} %broadcast_add_fusion), kind=kLoop, calls=%fused_computation | loop fusion | flops 196608 | bytes 794816 | tf_op jit(solution)/shard_map/div | solution.py:345
Async XLA Ops:
  0.0 105.9 %copy-start.2 = (f32[2]{0:T(128)S(1)}, f32[2]{0:T(128)}, u32[]{:S(2)}) copy-start(f32[2]{0:T(128)} %param.10) | copy-start | bytes 28
  0.0 105.9 %copy-start.1 = (f32[24]{0:T(128)S(1)}, f32[24]{0:T(128)}, u32[]{:S(2)}) copy-start(f32[24]{0:T(128)} %param.9) | copy-start | bytes 292
  0.0 106.0 %copy-start = (f32[2048]{0:T(1024)S(1)}, f32[2048]{0:T(1024)}, u32[]{:S(2)}) copy-start(f32[2048]{0:T(1024)} %param.11) | copy-start | bytes 24580

commit v5 on v4

--- a/solution.py
+++ b/solution.py
@@ -12,6 +12,7 @@
 NB = 2
 TILE = 128
 SLOTS = 128
+CAP = 8
 OUTS = 6
 GROUP = 4
 QUADS = 36
@@ -36,8 +37,10 @@
     i32 = jnp.int32
     square = (SLOTS, SLOTS)
     down, along = lax.broadcasted_iota(i32, square, 0), lax.broadcasted_iota(i32, square, 1)
-    out_along = jnp.broadcast_to(named[0:1, :], square)
-    out_down, amp_down = out_along.T, jnp.broadcast_to(named[1:2, :], square).T
+    out_of, amp_of = (jnp.concatenate([named[t, n : n + 1, :] for t in range(CAP)], axis=1) for n in range(2))
+    out_along = jnp.broadcast_to(out_of, square)
+    out_down, amp_down = out_along.T, jnp.broadcast_to(amp_of, square).T
+    tile_down = ((down & 15) << 3) + (down >> 4)
     same_before = jnp.where((out_along == out_down) & (along < down), 1, 0)
     rank = jnp.sum(same_before, axis=1, keepdims=True)
     start = jnp.zeros((1, SLOTS), i32)
@@ -54,12 +57,12 @@
     tiles, amps = [], []
     for g in range(GROUP):
         here = place == along * GROUP + g
-        tiles.append(SLOTS + jnp.sum(jnp.where(here, down - SLOTS, 0), axis=0, keepdims=True))
+        tiles.append(SLOTS + jnp.sum(jnp.where(here, tile_down - SLOTS, 0), axis=0, keepdims=True))
         amps.append(jnp.sum(jnp.where(here, amp_down, 0), axis=0, keepdims=True))
     return tiles + amps + [came_from, ends]
 
 
-def ladder_kernel(named, amps, tiles, owned, *scratch):
+def ladder_kernel(named, virt, b_level, pair, amps, tiles, owned, *scratch):
     slices = scratch[:SUBS]
     gathered = [ref.reshape(4, 2, 4, 4, ROWS, LANES) for ref in slices]
     (tiles_own, tiles_sib, history, part, relay, got1, sum1, got2, cross_out, cross_in, lists_out, lists_in, lists, lists_sib,
@@ -77,6 +80,13 @@
         place = list(at)
         place[axis] = turn(at[axis], by)
         return (place[Y] * 2 + core, place[Z] * RING + place[X])
+
+    square = (OWN, OWN)
+    diagonal = lax.broadcasted_iota(jnp.int32, square, 0) == lax.broadcasted_iota(jnp.int32, square, 1)
+    virt_down = jnp.sum(jnp.where(diagonal, jnp.broadcast_to(virt[...], square), 0.0), axis=1, keepdims=True)
+
+    def divided(total, b, columns):
+        return total / (virt_down + b_level[b] - pair[:, columns])
 
     partners = [peer(a, d) for a in (Y, Z, X) for d in (1, -1)] + [peer(a, 2) for a in (Y, Z, X)] + [sib]
     barrier = pltpu.get_barrier_semaphore()
@@ -260,7 +270,7 @@
                 cross_out[k, b] = total
             else:
                 columns = pl.ds(pl.multiple_of(core * (SUBS * LANES) + k * WIDE, WIDE), WIDE)
-                owned[b, :, columns] = total
+                owned[b, :, columns] = divided(total, b, columns)
         if g == 1:
             send(cross_out.at[k], cross_in.at[k], send_x.at[k], recv_x.at[k], sib)
 
@@ -268,7 +278,7 @@
         arrive(cross_in.at[k], send_x.at[k], recv_x.at[k], sib)
         for b in range(NB):
             columns = pl.ds(pl.multiple_of((1 - core) * (SUBS * LANES) + k * WIDE, WIDE), WIDE)
-            owned[b, :, columns] = cross_in[k, b]
+            owned[b, :, columns] = divided(cross_in[k, b], b, columns)
 
     def unit(work):
         return lambda n: work(n // 2, n % 2)
@@ -295,7 +305,7 @@
         copy.wait_send()
 
 
-def owned_ladder(named, amplitudes, tiles):
+def owned_update(named, virt, b_level, pair, amplitudes, tiles):
     dma = pltpu.SemaphoreType.DMA
     vmem = pltpu.VMEM
     f32 = jnp.float32
@@ -325,6 +335,9 @@
         out_shape=jax.ShapeDtypeStruct((NB, OWN, 2 * SUBS * LANES), f32),
         in_specs=[
             pl.BlockSpec(memory_space=pltpu.VMEM),
+            pl.BlockSpec(memory_space=pltpu.VMEM),
+            pl.BlockSpec(memory_space=pltpu.SMEM),
+            pl.BlockSpec(memory_space=pltpu.VMEM),
             pl.BlockSpec(memory_space=pl.ANY),
             pl.BlockSpec(memory_space=pl.ANY),
         ],
@@ -334,15 +347,13 @@
             collective_id=0, has_side_effects=True, vmem_limit_bytes=60 * 1024 * 1024
         ),
         name="ladder",
-    )(named, amplitudes, tiles)
+    )(named, virt, b_level, pair, amplitudes, tiles)
 
 
 def per_device(amplitudes, integrals, slot_index, virt_energy, b_energy, pair_energy):
-    named = slot_index.reshape(-1, 2).T
+    named = slot_index[0].transpose(1, 2, 0)
     tiles = integrals.reshape(-1, TILE, TILE)
-    owned = owned_ladder(named, amplitudes, tiles)
-    denom = virt_energy[None, :, None] + b_energy[:, None, None] - pair_energy[None, None, :]
-    return owned / denom
+    return owned_update(named, virt_energy[None, :], b_energy, pair_energy[None, :], amplitudes, tiles)
 
 
 def solution(mesh):

time: 108 us -> 107 us (level)
  other arithmetic: 1.94 us -> 0 us
    div x1 -> x0, other arithmetic: 1.87 us -> none  [per_device(): return owned / denom]
where the time goes in v5:
time: 107 us; the launch traced here: 106 us
  Pallas kernels  105 us (98%)
  local copies, waits for them, and re-layouts  1.77 us (2%)
    pallas_call x1, Pallas kernels, owned_update(): pl.pallas_call(ladder_kernel, out_shape=jax.ShapeDtypeStruct((NB, OWN, 2...  105 us

profile of v5, /device:TPU:1, one launch (start us, length us, event | category | flops | bytes accessed | tf_op | source)
XLA Modules:
  0.0 106.4 jit_solution(16810533252929213057)
XLA Ops:
  0.0 104.6 %ladder.1 = f32[2,24,2048]{2,1,0:T(8,128)} custom-call(s32[8,2,16]{2,1,0:T(2,128)} %bitcast.7, f32[1,24]{1,0:T(1,128)} %bitcast.9, f32[2]{0:T(128)} %b_level.1, f32[1,2048]{1,0:T(1,128)} %bitcast.8, bf16[48,2048]{1,0:T(8,128)(2,1)} %amps.1, bf16[128,128,128]{2,1,0:T(8,128)(2,1)} %bitcast.6), custom_call_target="tpu_custom_call" | custom-call | tf_op jit(solution)/shard_map/ladder/pallas_call | solution.py:333
  104.6 1.8 %copy.8 = f32[2,24,2048]{2,1,0:T(8,128)} copy(f32[2,24,2048]{2,1,0:T(8,128)} %ladder.1) | data formatting | bytes 786432

commit v6 on v5

--- a/solution.py
+++ b/solution.py
@@ -18,9 +18,11 @@
 QUADS = 36
 LANES = 128
 SUBS = 8
-CHUNKS = 4
-WIDE = LANES * SUBS // CHUNKS
+CHUNK_SUBS = ((0, 1), (2, 3), (4, 5), (6, 7))
+CHUNKS = len(CHUNK_SUBS)
+WIDE = 2 * LANES
 OWN = 24
+STEPS = 32000.0
 ROWS = 48
 RING = 4
 Y, Z, X = 0, 1, 2
@@ -30,6 +32,8 @@
     (Y, Z, X), (Y, X, Z),
     (X, Z, Y), (Z, X, Y),
 )
+AWAY = ((2, 2), (2, 1), (2, 3), (1, 2), (3, 2), (1, 1), (1, 3), (3, 1), (3, 3), (2, 0), (0, 2), (1, 0), (3, 0), (0, 1), (0, 3))
+FIRST = (0, 1, 3, 2, 4, 5, 6, 7)
 SUM_ORDERS = ((X, Z), (Z, X))
 
 
@@ -62,11 +66,42 @@
     return tiles + amps + [came_from, ends]
 
 
+def encode(ref, values):
+    powers = []
+    words = len(values) // 2
+    for j in range(words):
+        whole = []
+        for value in values[2 * j : 2 * j + 2]:
+            top = jnp.max(jnp.abs(value), axis=0, keepdims=True)
+            power = jnp.ceil(jnp.log2(jnp.maximum(top, 1e-30)))
+            whole.append(jnp.round(value * (STEPS * jnp.exp2(-power))).astype(jnp.int32))
+            powers.append(power)
+        ref[j * OWN : (j + 1) * OWN, :] = (whole[1] << 16) | (whole[0] & 0xFFFF)
+    while len(powers) < 8:
+        powers.append(powers[-1])
+    ref[words * OWN : words * OWN + 8, :] = jnp.concatenate(powers, axis=0).astype(jnp.int32)
+
+
+def decode(ref, blocks):
+    words = blocks // 2
+    scales = jnp.exp2(ref[words * OWN : words * OWN + 8, :].astype(jnp.float32)) * (1.0 / STEPS)
+    values = []
+    for j in range(words):
+        word = ref[j * OWN : (j + 1) * OWN, :]
+        values.append(((word << 16) >> 16).astype(jnp.float32) * scales[2 * j : 2 * j + 1, :])
+        values.append((word >> 16).astype(jnp.float32) * scales[2 * j + 1 : 2 * j + 2, :])
+    return values
+
+
+def message(blocks):
+    return pl.ds(0, blocks // 2 * OWN + 8)
+
+
 def ladder_kernel(named, virt, b_level, pair, amps, tiles, owned, *scratch):
     slices = scratch[:SUBS]
     gathered = [ref.reshape(4, 2, 4, 4, ROWS, LANES) for ref in slices]
-    (tiles_own, tiles_sib, history, part, relay, got1, sum1, got2, cross_out, cross_in, lists_out, lists_in, lists, lists_sib,
-     send0, recv0, local0, send_ag, recv_ag, send1, recv1, send2, recv2, send_x, recv_x, misc) = scratch[SUBS:]
+    (tiles_own, tiles_sib, history, part, far_out, near_out, mid_out, far_in, got1, sum1, next_out, got2, all_out, all_in, cross_out, cross_in, lists_out, lists_in, lists, lists_sib,
+     send0, recv0, local0, send_ag, recv_ag, send1, recv1, send2, recv2, send_x, recv_x, send_all, recv_all, misc) = scratch[SUBS:]
     row, col = lax.axis_index("row"), lax.axis_index("col")
     y, core = lax.div(row, 2), lax.rem(row, 2)
     z, x = lax.div(col, RING), lax.rem(col, RING)
@@ -108,15 +143,17 @@
             src_ref=dst, dst_ref=dst, send_sem=s_sem, recv_sem=r_sem, device_id=to, device_id_type=MESH
         ).wait_recv()
 
-    here = []
-    for s in range(SUBS):
+    steps = (1, -1, 2)
+
+    here = {}
+    for s in FIRST:
         mine = pl.ds(pl.multiple_of(core * (SUBS * LANES) + s * LANES, LANES), LANES)
         other = pl.ds(pl.multiple_of((1 - core) * (SUBS * LANES) + s * LANES, LANES), LANES)
         home = gathered[s].at[y, core, z, x]
         send(amps.at[:, other], home, send0.at[s], recv0.at[s], sib)
         copy = pltpu.make_async_copy(amps.at[:, mine], home, local0.at[s])
         copy.start()
-        here.append(copy)
+        here[s] = copy
     send(tiles, tiles_sib.at[pl.ds(0, SLOTS)], misc.at[2], misc.at[3], sib)
     own_tiles = pltpu.make_async_copy(tiles, tiles_own.at[pl.ds(0, SLOTS)], misc.at[4])
     own_tiles.start()
@@ -130,8 +167,6 @@
         pick = [slice(None) if a in done else at[a] for a in (Y, Z, X)]
         pick[axis] = index
         return gathered[s].at[pick[Y], half, pick[Z], pick[X]]
-
-    steps = (1, -1, 2)
 
     def spread(s, phase):
         axis = ORDERS[s][phase]
@@ -205,86 +240,128 @@
 
     def products(k, group):
         which, tile_ref = ((lists, tiles_own), (lists_sib, tiles_sib))[group]
-        per = SUBS // CHUNKS
-        parts = slices[k * per : (k + 1) * per]
+        subs = CHUNK_SUBS[k]
+        wide = len(subs) * LANES
 
         def step(q, carry):
             left, right = [], []
             for g in range(GROUP):
                 left.append(tile_ref[which[g, q]])
                 m = which[GROUP + g, q]
-                right.append(jnp.concatenate([ref[m] for ref in parts], axis=1))
+                right.append(jnp.concatenate([slices[s][m] for s in subs], axis=1))
             new = jnp.dot(
                 jnp.concatenate(left, axis=1), jnp.concatenate(right, axis=0), preferred_element_type=jnp.float32
             )
-            history[q + 1] = history[which[8, q]] + new
+            history[q + 1, :, :wide] = history[which[8, q], :, :wide] + new
             return carry
 
         lax.fori_loop(0, QUADS, step, 0, unroll=12)
-        rows_ref = part.at[k, group].reshape(OUTS * TILE, WIDE)
         for o in range(OUTS):
-            rows_ref[o * TILE : (o + 1) * TILE, :] = history[which[9, o]]
-
-    def block(k, g, b, axis, index):
-        return part.at[k, g, b, index] if axis == Z else part.at[k, g, b, :, index]
+            total = history[which[9, o], :, :wide]
+            for n, s in enumerate(subs):
+                rows_ref = part.at[s, group].reshape(OUTS * TILE, LANES)
+                rows_ref[o * TILE : (o + 1) * TILE, :] = total[:, n * LANES : (n + 1) * LANES]
+
+    def mine_of(k, g, b, axis, index):
+        return [
+            part[s, g, b, index, i] if axis == Z else part[s, g, b, i, index] for i in range(RING) for s in CHUNK_SUBS[k]
+        ]
 
     def sum_send(k, g):
         axis = SUM_ORDERS[g][0]
-        for way, by in enumerate((1, -1)):
-            far = block(k, g, way, axis, turn(at[axis], 2))
-            send(far, relay.at[k, g, way], send1.at[k, g, way], recv1.at[k, g, way], peer(axis, by))
-        for way, by in enumerate((1, -1)):
-            near = block(k, g, 1 - way, axis, turn(at[axis], by))
-            send(near, got1.at[k, g, way, 1 - way], send1.at[k, g, 2 + way], recv1.at[k, g, 2 + way], peer(axis, by))
+        rows = message(RING * len(CHUNK_SUBS[k]))
+        for way, by in enumerate((1, -1)):
+            encode(far_out.at[k, g, way], mine_of(k, g, way, axis, turn(at[axis], 2)))
+            send(far_out.at[k, g, way, rows], far_in.at[k, g, way, rows], send1.at[k, g, way], recv1.at[k, g, way], peer(axis, by))
+        for way, by in enumerate((1, -1)):
+            n = 2 + way
+            encode(near_out.at[k, g, way], mine_of(k, g, 1 - way, axis, turn(at[axis], by)))
+            send(near_out.at[k, g, way, rows], got1.at[k, g, way, 1 - way, rows], send1.at[k, g, n], recv1.at[k, g, n], peer(axis, by))
 
     def sum_relay(k, g):
         axis = SUM_ORDERS[g][0]
-        for way, by in enumerate((1, -1)):
-            arrive(relay.at[k, g, way], send1.at[k, g, way], recv1.at[k, g, way], peer(axis, by))
-            index = turn(at[axis], by)
-            for i in range(RING):
-                own = part[k, g, way, index, i] if axis == Z else part[k, g, way, i, index]
-                relay[k, g, way, i] = relay[k, g, way, i] + own
-            send(relay.at[k, g, way], got1.at[k, g, way, way], send1.at[k, g, 4 + way], recv1.at[k, g, 4 + way], peer(axis, by))
+        blocks = RING * len(CHUNK_SUBS[k])
+        rows = message(blocks)
+        for way, by in enumerate((1, -1)):
+            n = 4 + way
+            arrive(far_in.at[k, g, way, rows], send1.at[k, g, way], recv1.at[k, g, way], peer(axis, by))
+            own = mine_of(k, g, way, axis, turn(at[axis], by))
+            encode(mid_out.at[k, g, way], [a + b for a, b in zip(own, decode(far_in.at[k, g, way], blocks))])
+            send(mid_out.at[k, g, way, rows], got1.at[k, g, way, way, rows], send1.at[k, g, n], recv1.at[k, g, n], peer(axis, by))
 
     def sum_pass(k, g):
         axis, then = SUM_ORDERS[g]
+        subs = CHUNK_SUBS[k]
+        blocks = RING * len(subs)
+        rows = message(blocks)
         for way, by in enumerate((1, -1)):
             for n, b in ((2, 1 - way), (4, way)):
-                arrive(got1.at[k, g, way, b], send1.at[k, g, n + way], recv1.at[k, g, n + way], peer(axis, by))
+                arrive(got1.at[k, g, way, b, rows], send1.at[k, g, n + way], recv1.at[k, g, n + way], peer(axis, by))
         for b in range(NB):
-            for i in range(RING):
-                own = part[k, g, b, at[Z], i] if axis == Z else part[k, g, b, i, at[X]]
-                sum1[k, g, b, i] = own + (got1[k, g, 0, b, i] + got1[k, g, 1, b, i])
+            own = mine_of(k, g, b, axis, at[axis])
+            one, two = (decode(got1.at[k, g, way, b], blocks) for way in range(2))
+            for j in range(blocks):
+                sum1[subs[j % len(subs)], g, b, j // len(subs)] = own[j] + (one[j] + two[j])
+        rows = message(NB * len(subs))
         for n, by in enumerate(steps):
-            src = sum1.at[k, g, :, turn(at[then], by)]
-            send(src, got2.at[k, g, n], send2.at[k, g, n], recv2.at[k, g, n], peer(then, by))
+            index = turn(at[then], by)
+            encode(next_out.at[k, g, n], [sum1[s, g, b, index] for b in range(NB) for s in subs])
+            send(next_out.at[k, g, n, rows], got2.at[k, g, n, rows], send2.at[k, g, n], recv2.at[k, g, n], peer(then, by))
 
     def sum_end(k, g):
         then = SUM_ORDERS[g][1]
+        subs = CHUNK_SUBS[k]
+        blocks = NB * len(subs)
+        rows = message(blocks)
         for n, by in enumerate(steps):
-            arrive(got2.at[k, g, n], send2.at[k, g, n], recv2.at[k, g, n], peer(then, by))
-        for b in range(NB):
-            total = (sum1[k, g, b, at[then]] + got2[k, g, 0, b]) + (got2[k, g, 1, b] + got2[k, g, 2, b])
+            arrive(got2.at[k, g, n, rows], send2.at[k, g, n], recv2.at[k, g, n], peer(then, by))
+        got = [decode(got2.at[k, g, n], blocks) for n in range(3)]
+        own = [sum1[s, g, b, at[then]] for b in range(NB) for s in subs]
+        deliver(g, subs, [(own[j] + got[0][j]) + (got[1][j] + got[2][j]) for j in range(blocks)])
+
+    def all_send(k, g):
+        rows = message(NB * len(CHUNK_SUBS[k]))
+        for n, (dz, dx) in enumerate(AWAY):
+            to_z, to_x = turn(z, dz), turn(x, dx)
+            encode(all_out.at[g, n], [part[s, g, b, to_z, to_x] for b in range(NB) for s in CHUNK_SUBS[k]])
+            to = (row, to_z * RING + to_x)
+            send(all_out.at[g, n, rows], all_in.at[g, n, rows], send_all.at[g, n], recv_all.at[g, n], to)
+
+    def all_end(k, g):
+        subs = CHUNK_SUBS[k]
+        blocks = NB * len(subs)
+        rows = message(blocks)
+        totals = [part[s, g, b, z, x] for b in range(NB) for s in subs]
+        for n, (dz, dx) in enumerate(AWAY):
+            to = (row, turn(z, dz) * RING + turn(x, dx))
+            arrive(all_in.at[g, n, rows], send_all.at[g, n], recv_all.at[g, n], to)
+            totals = [a + b for a, b in zip(totals, decode(all_in.at[g, n], blocks))]
+        deliver(g, subs, totals)
+
+    def deliver(g, subs, totals):
+        for j, total in enumerate(totals):
+            b, s = j // len(subs), subs[j % len(subs)]
             if g == 1:
-                cross_out[k, b] = total
+                cross_out[s, b] = total
             else:
-                columns = pl.ds(pl.multiple_of(core * (SUBS * LANES) + k * WIDE, WIDE), WIDE)
+                columns = pl.ds(pl.multiple_of(core * (SUBS * LANES) + s * LANES, LANES), LANES)
                 owned[b, :, columns] = divided(total, b, columns)
         if g == 1:
-            send(cross_out.at[k], cross_in.at[k], send_x.at[k], recv_x.at[k], sib)
-
-    def sum_cross(k):
-        arrive(cross_in.at[k], send_x.at[k], recv_x.at[k], sib)
+            for s in subs:
+                send(cross_out.at[s], cross_in.at[s], send_x.at[s], recv_x.at[s], sib)
+
+    def sum_cross(s):
+        arrive(cross_in.at[s], send_x.at[s], recv_x.at[s], sib)
         for b in range(NB):
-            columns = pl.ds(pl.multiple_of((1 - core) * (SUBS * LANES) + k * WIDE, WIDE), WIDE)
-            owned[b, :, columns] = divided(cross_in[k, b], b, columns)
+            columns = pl.ds(pl.multiple_of((1 - core) * (SUBS * LANES) + s * LANES, LANES), LANES)
+            owned[b, :, columns] = divided(cross_in[s, b], b, columns)
 
     def unit(work):
         return lambda n: work(n // 2, n % 2)
 
     fwd, rest, done = last_forward, last_rest, last_finish
     mul, out, mid, add, end = (unit(w) for w in (products, sum_send, sum_relay, sum_pass, sum_end))
+    far_send, far_end = unit(all_send), unit(all_end)
     plan = [(first, s) for s in (0, 1, 3, 2)] + [(slots_sent, 0)] + [(second, s) for s in (0, 1, 3, 2)]
     plan += [(first, s) for s in (4, 5, 6, 7)] + [(third, s) for s in (0, 1, 3)]
     plan += [(second, s) for s in (6, 7, 4, 5)] + [(slots_ready, 0)]
@@ -299,8 +376,8 @@
     plan += [(mul, 7), (out, 7), (mid, 6), (add, 5), (end, 3), (mid, 7), (add, 6), (end, 4), (end, 5), (add, 7), (end, 6), (end, 7)]
     for work, which in plan:
         work(which)
-    for k in range(CHUNKS):
-        sum_cross(k)
+    for s in range(SUBS):
+        sum_cross(s)
     for copy in sent:
         copy.wait_send()
 
@@ -314,21 +391,27 @@
         vmem((SLOTS + 1, TILE, TILE), jnp.bfloat16),
         vmem((SLOTS + 1, TILE, TILE), jnp.bfloat16),
         vmem((QUADS + 1, TILE, WIDE), f32),
-        vmem((CHUNKS, 2, NB, RING, RING, OWN, WIDE), f32),
-        vmem((CHUNKS, 2, 2, RING, OWN, WIDE), f32),
-        vmem((CHUNKS, 2, 2, NB, RING, OWN, WIDE), f32),
-        vmem((CHUNKS, 2, NB, RING, OWN, WIDE), f32),
-        vmem((CHUNKS, 2, 3, NB, OWN, WIDE), f32),
-        vmem((CHUNKS, NB, OWN, WIDE), f32),
-        vmem((CHUNKS, NB, OWN, WIDE), f32),
+        vmem((SUBS, 2, NB, RING, RING, OWN, LANES), f32),
+        vmem((CHUNKS, 2, 2, RING * OWN + 8, LANES), jnp.int32),
+        vmem((CHUNKS, 2, 2, RING * OWN + 8, LANES), jnp.int32),
+        vmem((CHUNKS, 2, 2, RING * OWN + 8, LANES), jnp.int32),
+        vmem((CHUNKS, 2, 2, RING * OWN + 8, LANES), jnp.int32),
+        vmem((CHUNKS, 2, 2, NB, RING * OWN + 8, LANES), jnp.int32),
+        vmem((SUBS, 2, NB, RING, OWN, LANES), f32),
+        vmem((CHUNKS, 2, 3, NB * OWN + 8, LANES), jnp.int32),
+        vmem((CHUNKS, 2, 3, NB * OWN + 8, LANES), jnp.int32),
+        vmem((2, 15, NB // 2 * OWN + 8, LANES), jnp.int32),
+        vmem((2, 15, NB // 2 * OWN + 8, LANES), jnp.int32),
+        vmem((SUBS, NB, OWN, LANES), f32),
+        vmem((SUBS, NB, OWN, LANES), f32),
         vmem((16, 128), jnp.int32),
         vmem((16, 128), jnp.int32),
         pltpu.SMEM((16, 128), jnp.int32),
         pltpu.SMEM((16, 128), jnp.int32),
         dma((SUBS,)), dma((SUBS,)), dma((SUBS,)),
-        dma((SUBS, 12)), dma((SUBS, 12)),
+        dma((SUBS, 16)), dma((SUBS, 16)),
         dma((CHUNKS, 2, 6)), dma((CHUNKS, 2, 6)), dma((CHUNKS, 2, 3)), dma((CHUNKS, 2, 3)),
-        dma((CHUNKS,)), dma((CHUNKS,)), dma((8,)),
+        dma((SUBS,)), dma((SUBS,)), dma((2, 15)), dma((2, 15)), dma((8,)),
     ]
     return pl.pallas_call(
         ladder_kernel,

time: 107 us -> 104 us (0.972)
  Pallas kernels: 105 us -> 102 us
    pallas_call x1, Pallas kernels: 105 us -> 102 us  [owned_update(): pl.pallas_call(ladder_kernel, out_shape=jax.ShapeDtypeStruct((NB, OWN, 2...]
where the time goes in v6:
time: 104 us
  Pallas kernels  102 us (98%)
  local copies, waits for them, and re-layouts  1.77 us (2%)
    pallas_call x1, Pallas kernels, owned_update(): pl.pallas_call(ladder_kernel, out_shape=jax.ShapeDtypeStruct((NB, OWN, 2...  102 us

profile of v6, /device:TPU:1, one launch (start us, length us, event | category | flops | bytes accessed | tf_op | source)
XLA Modules:
  0.0 104.0 jit_solution(13559127622138446471)
XLA Ops:
  0.0 102.2 %ladder.1 = f32[2,24,2048]{2,1,0:T(8,128)} custom-call(s32[8,2,16]{2,1,0:T(2,128)} %bitcast.7, f32[1,24]{1,0:T(1,128)} %bitcast.9, f32[2]{0:T(128)} %b_level.1, f32[1,2048]{1,0:T(1,128)} %bitcast.8, bf16[48,2048]{1,0:T(8,128)(2,1)} %amps.1, bf16[128,128,128]{2,1,0:T(8,128)(2,1)} %bitcast.6), custom_call_target="tpu_custom_call" | custom-call | tf_op jit(solution)/shard_map/ladder/pallas_call | solution.py:416
  102.2 1.8 %copy.8 = f32[2,24,2048]{2,1,0:T(8,128)} copy(f32[2,24,2048]{2,1,0:T(8,128)} %ladder.1) | data formatting | bytes 786432
